TPU v7x, 256 devices: a whole 4x4x8 slice. The times are simulated.
256 devices in a mesh: dp: 16 (over x, z_lo, core), tensor: 16 (over z_hi, y).
Axes of the slice: x: 4, y: 4, z: 8 (z_hi: 4, z_lo: 2; z = z_hi * 2 + z_lo), core: 2. Of those that a mesh axis runs over, the one named last changes fastest.
Arguments:
- tokens: bfloat16 [32768, 3072], P(('dp', 'tensor')), may hold values from -6 to 6
- routes: int32 [32768, 2], P(('dp', 'tensor')), may hold values from 0 to 7, as said below
- router: bfloat16 [3072, 8], replicated, may hold values from -0.109375 to 0.109375
- w_up: bfloat16 [3072, 16384], P('dp', 'tensor'), may hold values from -0.109375 to 0.109375
- w_down: bfloat16 [16384, 3072], P(('tensor', 'dp')), may hold values from -0.046875 to 0.046875
- grad_parts: bfloat16 [16, 16384, 3072], P('dp', 'tensor'), may hold values from -6 to 6
- master: float32 [16384, 3072], P(('tensor', 'dp')), may hold values from -4 to 4
- moment_one: bfloat16 [16384, 3072], P(('tensor', 'dp')), may hold values from -3 to 3
- moment_two: float32 [16384, 3072], P(('tensor', 'dp')), may hold values from 0.01 to 1
Outputs:
- mixed: bfloat16 [32768, 3072], P(('dp', 'tensor'))
- new_master: float32 [16384, 3072], P(('tensor', 'dp'))
- new_moment_one: bfloat16 [16384, 3072], P(('tensor', 'dp'))
- new_moment_two: float32 [16384, 3072], P(('tensor', 'dp'))
Inputs may be any that keep to these rules, and one draw needn't show every extreme that they name: `routes`: each row names two different experts. Among the 128 rows of one device at most 48 name expert 0, and on some device exactly 48.
All inputs are finite; a program needn't handle non-finite values.
Results may differ from a plain program's by a relative error of at most 0.02.
Values may be sent and summed in bfloat16 or wider, within the bound.
No kernel may reach another device: no remote copies, remote signals or barrier semaphores. Data moves between devices by JAX's collectives and lax.ppermute only.
A program may use at most 128 MiB of HBM per device.

v0:
```python
import jax
import jax.numpy as jnp
from jax import lax
from jax.experimental import pallas as pl
from jax.experimental.pallas import tpu as pltpu
from jax.sharding import PartitionSpec as P

CAP = 48
D = 3072
N_X, N_ZL, N_C = 4, 2, 2
N_ZH, N_Y = 4, 4

beta_first = 0.9
beta_second = 0.999
learn_rate = 0.01
decay_rate = 0.1
adam_eps = 1e-08
bias_first = 1.0 - (0.9**10) ** 10
bias_second = 1.0 - (0.999**10) ** 10


def dp_of(x, zl, c):
    return (x % N_X) * 4 + (zl % N_ZL) * 2 + c % N_C


def tensor_of(zh, y):
    return (zh % N_ZH) * 4 + y % N_Y


def get_dp(value, x=0, zl=0, c=0):
    pairs = [
        (dp_of(i + x, j + zl, k + c), dp_of(i, j, k))
        for i in range(N_X)
        for j in range(N_ZL)
        for k in range(N_C)
    ]
    return lax.ppermute(value, "dp", pairs)


def get_tensor(value, zh=0, y=0):
    pairs = [(tensor_of(i + zh, j + y), tensor_of(i, j)) for i in range(N_ZH) for j in range(N_Y)]
    return lax.ppermute(value, "tensor", pairs)


def gating_of(tokens, routes, router):
    logits = jnp.dot(tokens, router, preferred_element_type=jnp.float32)
    expert_iota = jnp.arange(logits.shape[1], dtype=jnp.int32)
    chosen = jnp.sum(jnp.where(routes[:, :, None] == expert_iota, logits[:, None, :], 0.0), axis=2)
    is_first = routes[:, 0] == 0
    routed = is_first | (routes[:, 1] == 0)
    own_logit = jnp.where(is_first, chosen[:, 0], chosen[:, 1])
    partner = jnp.where(is_first, chosen[:, 1], chosen[:, 0])
    gating = jnp.where(routed, jax.nn.sigmoid(own_logit - partner), 0.0)
    return (routed, gating)


def adam_step(grad_total, master, moment_one, moment_two):
    new_one = (
        beta_first * moment_one.astype(jnp.float32) + (1.0 - beta_first) * grad_total
    ).astype(jnp.bfloat16)
    new_two = beta_second * moment_two + (1.0 - beta_second) * grad_total * grad_total
    update = new_one.astype(jnp.float32) / bias_first / (jnp.sqrt(new_two / bias_second) + adam_eps)
    new_master = master - learn_rate * (update + decay_rate * master)
    return (new_master, new_one, new_two)


def total(parts):
    acc = parts[0].astype(jnp.float32)
    for part in parts[1:]:
        acc = acc + part.astype(jnp.float32)
    return acc


VMEM = 40 << 20


def gelu(u):
    return 0.5 * u * (1.0 + lax.erf(u * 0.7071067811865476))


def up_kernel(y0, y1, y3, y2_left, y2_right, w, h):
    def put(at, u):
        h[at * 192 : (at + 1) * 192, :] = gelu(u).astype(jnp.bfloat16)

    for at, y in ((0, y0), (1, y1), (3, y3)):
        put(at, jnp.dot(y[...], w[...], preferred_element_type=jnp.float32))
    u = jnp.dot(y2_left[...], w[: D // 2], preferred_element_type=jnp.float32)
    put(2, u + jnp.dot(y2_right[...], w[D // 2 :], preferred_element_type=jnp.float32))


def up_call(rows, w):
    whole = lambda shape: pl.BlockSpec(shape, lambda n: (0, 0))
    return pl.pallas_call(
        up_kernel,
        out_shape=jax.ShapeDtypeStruct((768, 1024), jnp.bfloat16),
        grid=(4,),
        in_specs=[whole(r.shape) for r in rows] + [pl.BlockSpec((D, 256), lambda n: (0, n))],
        out_specs=pl.BlockSpec((768, 256), lambda n: (0, n)),
        compiler_params=pltpu.CompilerParams(vmem_limit_bytes=VMEM),
        cost_estimate=pl.CostEstimate(
            flops=2 * 768 * 1024 * D, bytes_accessed=2 * (768 * D + D * 1024 + 768 * 1024), transcendentals=0
        ),
        name="up",
    )(*rows, w)


def down_kernel(h, d, p0, p1, p2, p3):
    for at, p in ((2, p2), (1, p1), (3, p3), (0, p0)):
        rows = h[at * 192 : (at + 1) * 192, :]
        p[...] = jnp.dot(rows, d[...], preferred_element_type=jnp.float32).astype(jnp.bfloat16)


def down_call(h, d, first, width):
    at = first // width
    return pl.pallas_call(
        down_kernel,
        out_shape=[jax.ShapeDtypeStruct((192, 2 * width), jnp.bfloat16)] * 4,
        grid=(2,),
        in_specs=[
            pl.BlockSpec((768, 1024), lambda n: (0, 0)),
            pl.BlockSpec((1024, width), lambda n: (0, n + at)),
        ],
        out_specs=[pl.BlockSpec((192, width), lambda n: (0, n))] * 4,
        compiler_params=pltpu.CompilerParams(vmem_limit_bytes=VMEM),
        cost_estimate=pl.CostEstimate(
            flops=2 * 768 * 1024 * 2 * width, bytes_accessed=2 * (768 * 1024 + 1792 * 2 * width), transcendentals=0
        ),
        name="down",
    )(h, d)


def split_sum(parts, send):
    half = parts[0].shape[1] // 2
    left = send(parts[2][:, :half], 1)
    right = send(parts[2][:, half:], -1)
    ahead = jnp.concatenate(
        [total([parts[1][:, :half], left]).astype(jnp.bfloat16), parts[1][:, half:]], axis=1
    )
    behind = jnp.concatenate(
        [parts[3][:, :half], total([parts[3][:, half:], right]).astype(jnp.bfloat16)], axis=1
    )
    return total([parts[0], send(ahead, 1), send(behind, -1)])


def local(tokens, routes, router, w_up, w_down, grad_parts, master, moment_one, moment_two):
    here = lax.axis_index("dp")
    x, zl, c = here // 4, (here // 2) % 2, here % 2
    half = D // 2

    up = lax.all_gather(w_up, "dp", axis=0, tiled=True)
    down = lax.all_gather(w_down, "dp", axis=0, tiled=True)

    routed, gating = gating_of(tokens, routes, router)
    slot_index = jnp.cumsum(routed.astype(jnp.int32)) - 1
    slot_iota = jnp.arange(CAP, dtype=jnp.int32)
    picks = ((slot_index[None, :] == slot_iota[:, None]) & routed[None, :]).astype(jnp.bfloat16)
    own = jnp.dot(picks, tokens, preferred_element_type=jnp.float32).astype(jnp.bfloat16)
    near = [get_tensor(own, y=k) for k in (1, 3)]
    far = jnp.concatenate([get_tensor(own, zh=k) for k in (1, 3, 2)], axis=0)
    y0 = jnp.concatenate([own, far], axis=0)
    y1 = jnp.concatenate([near[0], get_tensor(far, y=1)], axis=0)
    y3 = jnp.concatenate([near[1], get_tensor(far, y=3)], axis=0)
    y2_left = get_tensor(y1[:, :half], y=1)
    y2_right = get_tensor(y3[:, half:], y=3)

    grads = grad_parts[0].reshape(8, 2, 64, D)
    keep = lax.dynamic_index_in_dim(grads, c, axis=1, keepdims=False)
    give = lax.dynamic_index_in_dim(grads, 1 - c, axis=1, keepdims=False)
    give, far_seen = lax.optimization_barrier((give, far))
    core_sum = total([keep, get_dp(give, c=1)]).astype(jnp.bfloat16).reshape(512, D)
    hidden = up_call((y0, y1, y3, y2_left, y2_right), up)
    core_sum, hidden = lax.optimization_barrier((core_sum, hidden))
    xgroups = [[dp_of(i, j, k) for i in range(N_X)] for j in range(N_ZL) for k in range(N_C)]
    x_sum = lax.psum_scatter(
        core_sum, "dp", scatter_dimension=0, tiled=True, axis_index_groups=xgroups
    ).reshape(2, 64, D)

    send_y = lambda value, k: get_tensor(value, y=-k)
    owned = []
    for first in (0, half):
        ysum = split_sum(down_call(hidden, down, first, half // 2), send_y)
        ysum = lax.optimization_barrier(ysum.astype(jnp.bfloat16)).reshape(4, CAP, half)
        came = [ysum[0]] + [get_tensor(ysum[i], zh=-k) for i, k in ((1, 1), (2, 3), (3, 2))]
        owned.append(total(came))
    owned = jnp.concatenate(owned, axis=1)
    combined = jnp.take(owned, jnp.clip(slot_index, 0, CAP - 1), axis=0)
    mixed = (combined * gating[:, None]).astype(jnp.bfloat16)

    keep = lax.dynamic_index_in_dim(x_sum, zl, axis=0, keepdims=False)
    give = lax.dynamic_index_in_dim(x_sum, 1 - zl, axis=0, keepdims=False)
    grad_total = total([keep, get_dp(give, zl=1)])
    new_master, new_one, new_two = adam_step(grad_total, master, moment_one, moment_two)
    return (mixed, new_master, new_one, new_two)


def solution(mesh):
    placed = (
        P(("dp", "tensor"), None),
        P(("dp", "tensor"), None),
        P(),
        P("dp", "tensor"),
        P(("tensor", "dp"), None),
        P("dp", "tensor", None),
        P(("tensor", "dp"), None),
        P(("tensor", "dp"), None),
        P(("tensor", "dp"), None),
    )
    return jax.shard_map(
        local,
        mesh=mesh,
        in_specs=placed,
        out_specs=(
            P(("dp", "tensor"), None),
            P(("tensor", "dp"), None),
            P(("tensor", "dp"), None),
            P(("tensor", "dp"), None),
        ),
        check_vma=False,
    )
```

profile of v0, /device:TPU:2, one launch (start us, length us, event | category | flops | bytes accessed | tf_op | source)
XLA Modules:
  0.0 209.5 jit_solution(9805266226954986129)
XLA Ops:
  10.4 6.4 %collective-permute-start = (bf16[48,3072]{1,0:T(8,128)(2,1)S(1)}, bf16[48,3072]{1,0:T(8,128)(2,1)S(1)}, u32[]{:S(2)}, u32[]{:S(2)}) collective-permute-start(bf16[48,3072]{1,0:T(8,128)(2,1)S(1)} %convolution_convert_fusion), channel_id=1, source_target_pairs={{4,0},{5,1},{6,2},{7,3},{8,4},{9,5},{10,6},{11,7},{12,8},{13,9},{1... | collective-permute-start | bytes 884744 | tf_op jit(solution)/shard_map/ppermute | solution.py:42
  16.8 3.8 %collective-permute-start.2 = (bf16[48,3072]{1,0:T(8,128)(2,1)S(1)}, bf16[48,3072]{1,0:T(8,128)(2,1)S(1)}, u32[]{:S(2)}, u32[]{:S(2)}) collective-permute-start(bf16[48,3072]{1,0:T(8,128)(2,1)S(1)} %convolution_convert_fusion), channel_id=1, source_target_pairs={{8,0},{9,1},{10,2},{11,3},{12,4},{13,5},{14,6},{15,7},{0,8},{1,9},... | collective-permute-start | bytes 884744 | tf_op jit(solution)/shard_map/ppermute | solution.py:42
  20.6 3.7 %dynamic-slice_bitcast_fusion = bf16[8,64,3072]{2,1,0:T(8,128)(2,1)} fusion(bf16[8,2,64,3072]{3,2,1,0:T(8,128)(2,1)} %bitcast.20, s32[]{:T(128)S(6)} %select_n.70), kind=kLoop, calls=%fused_computation.4 | loop fusion | bytes 6291460 | tf_op jit(solution)/shard_map/jit(dynamic_index_in_dim)/squeeze | solution.py:168
  24.4 17.7 %collective-permute-done = bf16[48,3072]{1,0:T(8,128)(2,1)S(1)} collective-permute-done((bf16[48,3072]{1,0:T(8,128)(2,1)S(1)}, bf16[48,3072]{1,0:T(8,128)(2,1)S(1)}, u32[]{:S(2)}, u32[]{:S(2)}) %collective-permute-start) | collective-permute-done | bytes 294944 | tf_op jit(solution)/shard_map/ppermute | solution.py:42
  44.4 3.0 %collective-permute-start.4 = (bf16[48,3072]{1,0:T(8,128)(2,1)S(1)}, bf16[48,3072]{1,0:T(8,128)(2,1)S(1)}, u32[]{:S(2)}, u32[]{:S(2)}) collective-permute-start(bf16[48,3072]{1,0:T(8,128)(2,1)S(1)} %convolution_convert_fusion), channel_id=1, source_target_pairs={{1,0},{2,1},{3,2},{0,3},{5,4},{6,5},{7,6},{4,7},{9,8},{10,9},{11,1... | collective-permute-start | bytes 884744 | tf_op jit(solution)/shard_map/ppermute | solution.py:42
  48.2 3.3 %collective-permute-start.5 = (bf16[144,3072]{1,0:T(8,128)(2,1)}, bf16[144,3072]{1,0:T(8,128)(2,1)S(1)}, u32[]{:S(2)}, u32[]{:S(2)}) collective-permute-start(bf16[144,3072]{1,0:T(8,128)(2,1)} %constant_dynamic-update-slice_fusion), channel_id=1, source_target_pairs={{1,0},{2,1},{3,2},{0,3},{5,4},{6,5},{7,6},{4,7},{9,8},{10,9},{11,1... | collective-permute-start | bytes 2654216 | tf_op jit(solution)/shard_map/ppermute | solution.py:42
  51.5 3.2 %collective-permute-done.4 = bf16[48,3072]{1,0:T(8,128)(2,1)S(1)} collective-permute-done((bf16[48,3072]{1,0:T(8,128)(2,1)S(1)}, bf16[48,3072]{1,0:T(8,128)(2,1)S(1)}, u32[]{:S(2)}, u32[]{:S(2)}) %collective-permute-start.4) | collective-permute-done | bytes 294944 | tf_op jit(solution)/shard_map/ppermute | solution.py:42
  54.8 3.8 %collective-permute-done.6 = bf16[48,3072]{1,0:T(8,128)(2,1)} collective-permute-done((bf16[48,3072]{1,0:T(8,128)(2,1)S(1)}, bf16[48,3072]{1,0:T(8,128)(2,1)}, u32[]{:S(2)}, u32[]{:S(2)}) %collective-permute-start.6) | collective-permute-done | bytes 294944 | tf_op jit(solution)/shard_map/ppermute | solution.py:42
  58.6 1.0 constant_dynamic-update-slice_fusion.6
  59.6 1.1 pad_maximum_fusion.y0
  60.7 12.7 %collective-permute-done.5 = bf16[144,3072]{1,0:T(8,128)(2,1)S(1)} collective-permute-done((bf16[144,3072]{1,0:T(8,128)(2,1)}, bf16[144,3072]{1,0:T(8,128)(2,1)S(1)}, u32[]{:S(2)}, u32[]{:S(2)}) %collective-permute-start.5) | collective-permute-done | bytes 884768 | tf_op jit(solution)/shard_map/ppermute | solution.py:42
  73.5 3.7 %collective-permute-start.8 = (bf16[192,1536]{1,0:T(8,128)(2,1)S(1)}, bf16[192,1536]{1,0:T(8,128)(2,1)S(1)}, u32[]{:S(2)}, u32[]{:S(2)}) collective-permute-start(bf16[192,1536]{1,0:T(8,128)(2,1)S(1)} %slice.116), channel_id=1, source_target_pairs={{1,0},{2,1},{3,2},{0,3},{5,4},{6,5},{7,6},{4,7},{9,8},{10,9},{11,1... | collective-permute-start | bytes 1769480 | tf_op jit(solution)/shard_map/ppermute | solution.py:42
  77.6 5.7 %fusion = bf16[8,64,3072]{2,1,0:T(8,128)(2,1)} fusion(bf16[8,64,3072]{2,1,0:T(8,128)(2,1)} %collective-permute-done.3, bf16[8,2,64,3072]{3,2,1,0:T(8,128)(2,1)} %bitcast.21, s32[]{:T(128)S(6)} %select_n.69), kind=kLoop, calls=%fused_computation.2 | loop fusion | flops 6291456 | bytes 9437188 | tf_op jit(solution)/shard_map/convert_element_type | solution.py:170
  83.3 6.4 %collective-permute-done.8.y2_left = bf16[192,1536]{1,0:T(8,128)(2,1)S(1)} collective-permute-done((bf16[192,1536]{1,0:T(8,128)(2,1)S(1)}, bf16[192,1536]{1,0:T(8,128)(2,1)S(1)}, u32[]{:S(2)}, u32[]{:S(2)}) %collective-permute-start.8) | collective-permute-done | bytes 589856 | tf_op jit(solution)/shard_map/ppermute | solution.py:42
  89.7 0.8 copy-done.4
  90.5 3.0 %collective-permute-done.9.y2_right = bf16[192,1536]{1,0:T(8,128)(2,1)S(1)} collective-permute-done((bf16[192,1536]{1,0:T(8,128)(2,1)S(1)}, bf16[192,1536]{1,0:T(8,128)(2,1)S(1)}, u32[]{:S(2)}, u32[]{:S(2)}) %collective-permute-start.9) | collective-permute-done | bytes 589856 | tf_op jit(solution)/shard_map/ppermute | solution.py:42
  93.5 0.8 copy-done.6
  94.3 2.9 %copy-done.3 = bf16[3072,1024]{1,0:T(8,128)(2,1)S(1)} copy-done((bf16[3072,1024]{1,0:T(8,128)(2,1)S(1)}, bf16[3072,1024]{1,0:T(8,128)(2,1)}, u32[]{:S(2)}) %copy-start.3) | copy-done | bytes 6291480
  97.2 1.1 copy-done.5
  98.3 1.1 copy-done.7
  99.4 6.7 %up.1.h = bf16[768,1024]{1,0:T(8,128)(2,1)S(1)} custom-call(bf16[192,3072]{1,0:T(8,128)(2,1)S(1)} %pad_maximum_fusion.y0, bf16[192,3072]{1,0:T(8,128)(2,1)S(1)} %constant_dynamic-update-slice_fusion.3.y1, bf16[192,3072]{1,0:T(8,128)(2,1)S(1)} %constant_dynamic-update-slice_fusion.5.y3, bf16[192,1536]{1,0:T(8,128)(2,1)S(1)} %copy-done.5, ...), custom_call_target="tpu_custom_call" | custom-call | flops 4831838208 | bytes 12582912 | tf_op jit(solution)/shard_map/up/pallas_call | solution.py:93
  106.1 1.2 copy-done.8
  107.3 12.6 %all-gather.5.cloned.1.call-done.d = bf16[1024,3072]{1,0:T(8,128)(2,1)} async-done(((bf16[64,3072]{1,0:T(8,128)(2,1)}), bf16[1024,3072]{1,0:T(8,128)(2,1)}) %all-gather.5.cloned.1.call-update) | async-done | bytes 6291472 | tf_op jit(solution)/shard_map/all_gather | solution.py:151
  119.9 2.8 %copy-done.2 = bf16[1024,3072]{1,0:T(8,128)(2,1)S(1)} copy-done((bf16[1024,3072]{1,0:T(8,128)(2,1)S(1)}, bf16[1024,3072]{1,0:T(8,128)(2,1)}, u32[]{:S(2)}) %copy-start.2) | copy-done | bytes 6291480
  122.7 3.2 %down.2 = (bf16[192,1536]{1,0:T(8,128)(2,1)S(1)}, bf16[192,1536]{1,0:T(8,128)(2,1)S(1)}, bf16[192,1536]{1,0:T(8,128)(2,1)S(1)}, bf16[192,1536]{1,0:T(8,128)(2,1)S(1)}) custom-call(bf16[768,1024]{1,0:T(8,128)(2,1)S(1)} %copy-done.9, bf16[1024,3072]{1,0:T(8,128)(2,1)S(1)} %copy-done.2), custom_call_target="tpu_custom_call" | custom-call | flops 2415919104 | bytes 7077888 | tf_op jit(solution)/shard_map/down/pallas_call | solution.py:115
  125.9 1.6 collective-permute-start.10
  127.5 1.8 collective-permute-start.12
  129.3 3.2 %down.3 = (bf16[192,1536]{1,0:T(8,128)(2,1)S(1)}, bf16[192,1536]{1,0:T(8,128)(2,1)S(1)}, bf16[192,1536]{1,0:T(8,128)(2,1)S(1)}, bf16[192,1536]{1,0:T(8,128)(2,1)S(1)}) custom-call(bf16[768,1024]{1,0:T(8,128)(2,1)S(1)} %copy-done.9, bf16[1024,3072]{1,0:T(8,128)(2,1)S(1)} %copy-done.2), custom_call_target="tpu_custom_call" | custom-call | flops 2415919104 | bytes 7077888 | tf_op jit(solution)/shard_map/down/pallas_call | solution.py:115
  133.0 3.0 %collective-permute-start.19 = (bf16[192,768]{1,0:T(8,128)(2,1)S(1)}, bf16[192,768]{1,0:T(8,128)(2,1)S(1)}, u32[]{:S(2)}, u32[]{:S(2)}) collective-permute-start(bf16[192,768]{1,0:T(8,128)(2,1)S(1)} %get-tuple-element.40), channel_id=1, source_target_pairs={{1,0},{2,1},{3,2},{0,3},{5,4},{6,5},{7,6},{4,7},{9,8},{10,9},{11,1... | collective-permute-start | bytes 884744 | tf_op jit(solution)/shard_map/ppermute | solution.py:42
  136.6 0.9 collective-permute-start.11
  137.7 2.5 %collective-permute-start.13 = (bf16[192,1536]{1,0:T(8,128)(2,1)S(1)}, bf16[192,1536]{1,0:T(8,128)(2,1)S(1)}, u32[]{:S(2)}, u32[]{:S(2)}) collective-permute-start(bf16[192,1536]{1,0:T(8,128)(2,1)S(1)} %pad_maximum_fusion.2), channel_id=1, source_target_pairs={{1,0},{2,1},{3,2},{0,3},{5,4},{6,5},{7,6},{4,7},{9,8},{10,9},{11,1... | collective-permute-start | bytes 1769480 | tf_op jit(solution)/shard_map/ppermute | solution.py:42
  140.1 3.7 %collective-permute-done.17 = bf16[192,768]{1,0:T(8,128)(2,1)S(1)} collective-permute-done((bf16[192,768]{1,0:T(8,128)(2,1)S(1)}, bf16[192,768]{1,0:T(8,128)(2,1)S(1)}, u32[]{:S(2)}, u32[]{:S(2)}) %collective-permute-start.17) | collective-permute-done | bytes 294944 | tf_op jit(solution)/shard_map/ppermute | solution.py:42
  144.2 3.5 %collective-permute-start.20 = (bf16[192,1536]{1,0:T(8,128)(2,1)S(1)}, bf16[192,1536]{1,0:T(8,128)(2,1)S(1)}, u32[]{:S(2)}, u32[]{:S(2)}) collective-permute-start(bf16[192,1536]{1,0:T(8,128)(2,1)S(1)} %pad_maximum_fusion.4), channel_id=1, source_target_pairs={{1,0},{2,1},{3,2},{0,3},{5,4},{6,5},{7,6},{4,7},{9,8},{10,9},{11,1... | collective-permute-start | bytes 1769480 | tf_op jit(solution)/shard_map/ppermute | solution.py:42
  147.7 8.8 %collective-permute-done.11 = bf16[192,1536]{1,0:T(8,128)(2,1)S(1)} collective-permute-done((bf16[192,1536]{1,0:T(8,128)(2,1)S(1)}, bf16[192,1536]{1,0:T(8,128)(2,1)S(1)}, u32[]{:S(2)}, u32[]{:S(2)}) %collective-permute-start.11) | collective-permute-done | bytes 589856 | tf_op jit(solution)/shard_map/ppermute | solution.py:42
  156.7 2.6 %collective-permute-start.14 = (bf16[48,1536]{1,0:T(8,128)(2,1)S(1)}, bf16[48,1536]{1,0:T(8,128)(2,1)S(1)}, u32[]{:S(2)}, u32[]{:S(2)}) collective-permute-start(bf16[48,1536]{1,0:T(8,128)(2,1)S(1)} %get-tuple-element.31), channel_id=1, source_target_pairs={{12,0},{13,1},{14,2},{15,3},{0,4},{1,5},{2,6},{3,7},{4,8},{5,9},{6... | collective-permute-start | bytes 442376 | tf_op jit(solution)/shard_map/ppermute | solution.py:42
  159.3 1.7 collective-permute-start.15
  161.0 5.7 %collective-permute-start.16 = (bf16[48,1536]{1,0:T(8,128)(2,1)S(1)}, bf16[48,1536]{1,0:T(8,128)(2,1)S(1)}, u32[]{:S(2)}, u32[]{:S(2)}) collective-permute-start(bf16[48,1536]{1,0:T(8,128)(2,1)S(1)} %get-tuple-element.32), channel_id=1, source_target_pairs={{8,0},{9,1},{10,2},{11,3},{12,4},{13,5},{14,6},{15,7},{0,8},{1,9},... | collective-permute-start | bytes 442376 | tf_op jit(solution)/shard_map/ppermute | solution.py:42
  166.7 1.3 collective-permute-done.18
  168.3 2.6 %collective-permute-start.21 = (bf16[48,1536]{1,0:T(8,128)(2,1)S(1)}, bf16[48,1536]{1,0:T(8,128)(2,1)S(1)}, u32[]{:S(2)}, u32[]{:S(2)}) collective-permute-start(bf16[48,1536]{1,0:T(8,128)(2,1)S(1)} %get-tuple-element.36), channel_id=1, source_target_pairs={{12,0},{13,1},{14,2},{15,3},{0,4},{1,5},{2,6},{3,7},{4,8},{5,9},{6... | collective-permute-start | bytes 442376 | tf_op jit(solution)/shard_map/ppermute | solution.py:42
  170.9 1.7 collective-permute-start.22
  172.6 5.7 %collective-permute-start.23 = (bf16[48,1536]{1,0:T(8,128)(2,1)S(1)}, bf16[48,1536]{1,0:T(8,128)(2,1)S(1)}, u32[]{:S(2)}, u32[]{:S(2)}) collective-permute-start(bf16[48,1536]{1,0:T(8,128)(2,1)S(1)} %get-tuple-element.37), channel_id=1, source_target_pairs={{8,0},{9,1},{10,2},{11,3},{12,4},{13,5},{14,6},{15,7},{0,8},{1,9},... | collective-permute-start | bytes 442376 | tf_op jit(solution)/shard_map/ppermute | solution.py:42
  178.4 9.5 %collective-permute-done.22 = bf16[48,1536]{1,0:T(8,128)(2,1)S(1)} collective-permute-done((bf16[48,1536]{1,0:T(8,128)(2,1)S(1)}, bf16[48,1536]{1,0:T(8,128)(2,1)S(1)}, u32[]{:S(2)}, u32[]{:S(2)}) %collective-permute-start.22) | collective-permute-done | bytes 147488 | tf_op jit(solution)/shard_map/ppermute | solution.py:42
  188.0 1.2 gather_fusion
  189.2 1.1 dynamic-slice_bitcast_fusion.1
  190.3 2.0 collective-permute-start.24
  192.3 1.1 multiply_convert_fusion
  193.4 7.8 %collective-permute-done.24 = bf16[64,3072]{1,0:T(8,128)(2,1)S(1)} collective-permute-done((bf16[64,3072]{1,0:T(8,128)(2,1)S(1)}, bf16[64,3072]{1,0:T(8,128)(2,1)S(1)}, u32[]{:S(2)}, u32[]{:S(2)}) %collective-permute-start.24) | collective-permute-done | bytes 393248 | tf_op jit(solution)/shard_map/ppermute | solution.py:37
  201.2 1.7 multiply_subtract_fusion
  (110 shorter events, 9.1 us)
Async XLA Ops:
  7.2 3.0 %copy-start = (bf16[128,3072]{1,0:T(8,128)(2,1)S(1)}, bf16[128,3072]{1,0:T(8,128)(2,1)}, u32[]{:S(2)}) copy-start(bf16[128,3072]{1,0:T(8,128)(2,1)} %param.9) | copy-start | bytes 2359300
  7.2 87.1 %all-gather.3.cloned.1.call-start = ((), (), s32[]{:S(2)}) async-start(), calls=%async_computation.1 | async-start | bytes 6684672 | tf_op jit(solution)/shard_map/all_gather | solution.py:150
  7.9 112.0 %all-gather.5.cloned.1.call-start = ((), (), s32[]{:S(2)}) async-start(), calls=%async_computation.2 | async-start | bytes 6684672 | tf_op jit(solution)/shard_map/all_gather | solution.py:151
  8.7 180.5 %reduce-scatter.2.cloned.1.call-start = ((), (), s32[]{:S(2)}) async-start(), calls=%async_computation.3 | async-start | bytes 3932160 | tf_op jit(solution)/shard_map/reduce_scatter | solution.py:174
  10.4 37.0 %copy-start.10 = (bf16[48,3072]{1,0:T(8,128)(2,1)}, bf16[48,3072]{1,0:T(8,128)(2,1)S(1)}, u32[]{:S(2)}) copy-start(bf16[48,3072]{1,0:T(8,128)(2,1)S(1)} %convolution_convert_fusion) | copy-start | bytes 884740
  10.4 31.6 %collective-permute-start = (bf16[48,3072]{1,0:T(8,128)(2,1)S(1)}, bf16[48,3072]{1,0:T(8,128)(2,1)S(1)}, u32[]{:S(2)}, u32[]{:S(2)}) collective-permute-start(bf16[48,3072]{1,0:T(8,128)(2,1)S(1)} %convolution_convert_fusion), channel_id=1, source_target_pairs={{4,0},{5,1},{6,2},{7,3},{8,4},{9,5},{10,6},{11,7},{12,8},{13,9},{1... | collective-permute-start | bytes 884744 | tf_op jit(solution)/shard_map/ppermute | solution.py:42
  16.8 26.1 %collective-permute-start.1 = (bf16[48,3072]{1,0:T(8,128)(2,1)S(1)}, bf16[48,3072]{1,0:T(8,128)(2,1)S(1)}, u32[]{:S(2)}, u32[]{:S(2)}) collective-permute-start(bf16[48,3072]{1,0:T(8,128)(2,1)S(1)} %convolution_convert_fusion), channel_id=1, source_target_pairs={{12,0},{13,1},{14,2},{15,3},{0,4},{1,5},{2,6},{3,7},{4,8},{5,9},{6... | collective-permute-start | bytes 884744 | tf_op jit(solution)/shard_map/ppermute | solution.py:42
  16.8 26.8 %collective-permute-start.2 = (bf16[48,3072]{1,0:T(8,128)(2,1)S(1)}, bf16[48,3072]{1,0:T(8,128)(2,1)S(1)}, u32[]{:S(2)}, u32[]{:S(2)}) collective-permute-start(bf16[48,3072]{1,0:T(8,128)(2,1)S(1)} %convolution_convert_fusion), channel_id=1, source_target_pairs={{8,0},{9,1},{10,2},{11,3},{12,4},{13,5},{14,6},{15,7},{0,8},{1,9},... | collective-permute-start | bytes 884744 | tf_op jit(solution)/shard_map/ppermute | solution.py:42
  24.4 23.1 %copy-start.20 = (bf16[3072,8]{0,1:T(8,128)(2,1)S(1)}, bf16[3072,8]{0,1:T(8,128)(2,1)}, u32[]{:S(2)}) copy-start(bf16[3072,8]{0,1:T(8,128)(2,1)} %param.11) | copy-start | bytes 147460
  42.1 5.7 %copy-start.11 = (bf16[48,3072]{1,0:T(8,128)(2,1)}, bf16[48,3072]{1,0:T(8,128)(2,1)S(1)}, u32[]{:S(2)}) copy-start(bf16[48,3072]{1,0:T(8,128)(2,1)S(1)} %collective-permute-done) | copy-start | bytes 884740
  42.9 4.9 %copy-start.21 = (s32[128,2]{0,1:T(2,128)S(1)}, s32[128,2]{0,1:T(2,128)}, u32[]{:S(2)}) copy-start(s32[128,2]{0,1:T(2,128)} %param.10) | copy-start | bytes 3076
  42.9 5.3 %copy-start.13 = (bf16[48,3072]{1,0:T(8,128)(2,1)}, bf16[48,3072]{1,0:T(8,128)(2,1)S(1)}, u32[]{:S(2)}) copy-start(bf16[48,3072]{1,0:T(8,128)(2,1)S(1)} %collective-permute-done.1) | copy-start | bytes 884740
  43.6 11.2 %copy-start.15 = (bf16[48,3072]{1,0:T(8,128)(2,1)}, bf16[48,3072]{1,0:T(8,128)(2,1)S(1)}, u32[]{:S(2)}) copy-start(bf16[48,3072]{1,0:T(8,128)(2,1)S(1)} %collective-permute-done.2) | copy-start | bytes 884740
  44.4 33.2 %collective-permute-start.3 = (bf16[8,64,3072]{2,1,0:T(8,128)(2,1)}, bf16[8,64,3072]{2,1,0:T(8,128)(2,1)}, u32[]{:S(2)}, u32[]{:S(2)}) collective-permute-start(bf16[8,64,3072]{2,1,0:T(8,128)(2,1)} %dynamic-slice_bitcast_fusion), channel_id=1, source_target_pairs={{16,0},{0,16},{48,32},{32,48},{80,64},{64,80},{112,96},{96,112},{1... | collective-permute-start | bytes 9437192 | tf_op jit(solution)/shard_map/ppermute | solution.py:37
  44.4 10.3 %collective-permute-start.4 = (bf16[48,3072]{1,0:T(8,128)(2,1)S(1)}, bf16[48,3072]{1,0:T(8,128)(2,1)S(1)}, u32[]{:S(2)}, u32[]{:S(2)}) collective-permute-start(bf16[48,3072]{1,0:T(8,128)(2,1)S(1)} %convolution_convert_fusion), channel_id=1, source_target_pairs={{1,0},{2,1},{3,2},{0,3},{5,4},{6,5},{7,6},{4,7},{9,8},{10,9},{11,1... | collective-permute-start | bytes 884744 | tf_op jit(solution)/shard_map/ppermute | solution.py:42
  47.4 11.2 %collective-permute-start.6 = (bf16[48,3072]{1,0:T(8,128)(2,1)S(1)}, bf16[48,3072]{1,0:T(8,128)(2,1)}, u32[]{:S(2)}, u32[]{:S(2)}) collective-permute-start(bf16[48,3072]{1,0:T(8,128)(2,1)S(1)} %convolution_convert_fusion), channel_id=1, source_target_pairs={{3,0},{0,1},{1,2},{2,3},{7,4},{4,5},{5,6},{6,7},{11,8},{8,9},{9,10... | collective-permute-start | bytes 884744 | tf_op jit(solution)/shard_map/ppermute | solution.py:42
  48.0 11.5 %copy-start.12 = (bf16[48,3072]{1,0:T(8,128)(2,1)S(1)}, bf16[48,3072]{1,0:T(8,128)(2,1)}, u32[]{:S(2)}) copy-start(bf16[48,3072]{1,0:T(8,128)(2,1)} %copy-done.11) | copy-start | bytes 884740
  48.2 11.4 %copy-start.14 = (bf16[48,3072]{1,0:T(8,128)(2,1)S(1)}, bf16[48,3072]{1,0:T(8,128)(2,1)}, u32[]{:S(2)}) copy-start(bf16[48,3072]{1,0:T(8,128)(2,1)} %copy-done.13) | copy-start | bytes 884740
  48.2 25.2 %collective-permute-start.5 = (bf16[144,3072]{1,0:T(8,128)(2,1)}, bf16[144,3072]{1,0:T(8,128)(2,1)S(1)}, u32[]{:S(2)}, u32[]{:S(2)}) collective-permute-start(bf16[144,3072]{1,0:T(8,128)(2,1)} %constant_dynamic-update-slice_fusion), channel_id=1, source_target_pairs={{1,0},{2,1},{3,2},{0,3},{5,4},{6,5},{7,6},{4,7},{9,8},{10,9},{11,1... | collective-permute-start | bytes 2654216 | tf_op jit(solution)/shard_map/ppermute | solution.py:42
  51.5 25.7 %collective-permute-start.7 = (bf16[144,3072]{1,0:T(8,128)(2,1)}, bf16[144,3072]{1,0:T(8,128)(2,1)S(1)}, u32[]{:S(2)}, u32[]{:S(2)}) collective-permute-start(bf16[144,3072]{1,0:T(8,128)(2,1)} %constant_dynamic-update-slice_fusion), channel_id=1, source_target_pairs={{3,0},{0,1},{1,2},{2,3},{7,4},{4,5},{5,6},{6,7},{11,8},{8,9},{9,10... | collective-permute-start | bytes 2654216 | tf_op jit(solution)/shard_map/ppermute | solution.py:42
  73.5 16.1 %collective-permute-start.8 = (bf16[192,1536]{1,0:T(8,128)(2,1)S(1)}, bf16[192,1536]{1,0:T(8,128)(2,1)S(1)}, u32[]{:S(2)}, u32[]{:S(2)}) collective-permute-start(bf16[192,1536]{1,0:T(8,128)(2,1)S(1)} %slice.116), channel_id=1, source_target_pairs={{1,0},{2,1},{3,2},{0,3},{5,4},{6,5},{7,6},{4,7},{9,8},{10,9},{11,1... | collective-permute-start | bytes 1769480 | tf_op jit(solution)/shard_map/ppermute | solution.py:42
  77.3 16.1 %collective-permute-start.9 = (bf16[192,1536]{1,0:T(8,128)(2,1)S(1)}, bf16[192,1536]{1,0:T(8,128)(2,1)S(1)}, u32[]{:S(2)}, u32[]{:S(2)}) collective-permute-start(bf16[192,1536]{1,0:T(8,128)(2,1)S(1)} %slice.117), channel_id=1, source_target_pairs={{3,0},{0,1},{1,2},{2,3},{7,4},{4,5},{5,6},{6,7},{11,8},{8,9},{9,10... | collective-permute-start | bytes 1769480 | tf_op jit(solution)/shard_map/ppermute | solution.py:42
  94.3 2.9 %copy-start.3 = (bf16[3072,1024]{1,0:T(8,128)(2,1)S(1)}, bf16[3072,1024]{1,0:T(8,128)(2,1)}, u32[]{:S(2)}) copy-start(bf16[3072,1024]{1,0:T(8,128)(2,1)} %all-gather.3.cloned.1.call-done.w) | copy-start | bytes 18874372
  97.2 1.1 copy-start.5
  98.3 1.1 copy-start.7
  106.1 1.2 copy-start.8
  107.3 12.6 %copy-start.9 = (bf16[768,1024]{1,0:T(8,128)(2,1)S(1)}, bf16[768,1024]{1,0:T(8,128)(2,1)}, u32[]{:S(2)}) copy-start(bf16[768,1024]{1,0:T(8,128)(2,1)} %copy-done.8) | copy-start | bytes 4718596
  119.9 2.8 %copy-start.2 = (bf16[1024,3072]{1,0:T(8,128)(2,1)S(1)}, bf16[1024,3072]{1,0:T(8,128)(2,1)}, u32[]{:S(2)}) copy-start(bf16[1024,3072]{1,0:T(8,128)(2,1)} %all-gather.5.cloned.1.call-done.d) | copy-start | bytes 18874372
  125.9 10.6 %collective-permute-start.10 = (bf16[192,768]{1,0:T(8,128)(2,1)S(1)}, bf16[192,768]{1,0:T(8,128)(2,1)S(1)}, u32[]{:S(2)}, u32[]{:S(2)}) collective-permute-start(bf16[192,768]{1,0:T(8,128)(2,1)S(1)} %get-tuple-element.34), channel_id=1, source_target_pairs={{3,0},{0,1},{1,2},{2,3},{7,4},{4,5},{5,6},{6,7},{11,8},{8,9},{9,10... | collective-permute-start | bytes 884744 | tf_op jit(solution)/shard_map/ppermute | solution.py:42
  127.5 10.0 %collective-permute-start.12 = (bf16[192,768]{1,0:T(8,128)(2,1)S(1)}, bf16[192,768]{1,0:T(8,128)(2,1)S(1)}, u32[]{:S(2)}, u32[]{:S(2)}) collective-permute-start(bf16[192,768]{1,0:T(8,128)(2,1)S(1)} %get-tuple-element.35), channel_id=1, source_target_pairs={{1,0},{2,1},{3,2},{0,3},{5,4},{6,5},{7,6},{4,7},{9,8},{10,9},{11,1... | collective-permute-start | bytes 884744 | tf_op jit(solution)/shard_map/ppermute | solution.py:42
  132.6 11.2 %collective-permute-start.17 = (bf16[192,768]{1,0:T(8,128)(2,1)S(1)}, bf16[192,768]{1,0:T(8,128)(2,1)S(1)}, u32[]{:S(2)}, u32[]{:S(2)}) collective-permute-start(bf16[192,768]{1,0:T(8,128)(2,1)S(1)} %get-tuple-element.39), channel_id=1, source_target_pairs={{3,0},{0,1},{1,2},{2,3},{7,4},{4,5},{5,6},{6,7},{11,8},{8,9},{9,10... | collective-permute-start | bytes 884744 | tf_op jit(solution)/shard_map/ppermute | solution.py:42
  133.0 11.1 %collective-permute-start.19 = (bf16[192,768]{1,0:T(8,128)(2,1)S(1)}, bf16[192,768]{1,0:T(8,128)(2,1)S(1)}, u32[]{:S(2)}, u32[]{:S(2)}) collective-permute-start(bf16[192,768]{1,0:T(8,128)(2,1)S(1)} %get-tuple-element.40), channel_id=1, source_target_pairs={{1,0},{2,1},{3,2},{0,3},{5,4},{6,5},{7,6},{4,7},{9,8},{10,9},{11,1... | collective-permute-start | bytes 884744 | tf_op jit(solution)/shard_map/ppermute | solution.py:42
  136.6 19.9 %collective-permute-start.11 = (bf16[192,1536]{1,0:T(8,128)(2,1)S(1)}, bf16[192,1536]{1,0:T(8,128)(2,1)S(1)}, u32[]{:S(2)}, u32[]{:S(2)}) collective-permute-start(bf16[192,1536]{1,0:T(8,128)(2,1)S(1)} %pad_maximum_fusion.1), channel_id=1, source_target_pairs={{3,0},{0,1},{1,2},{2,3},{7,4},{4,5},{5,6},{6,7},{11,8},{8,9},{9,10... | collective-permute-start | bytes 1769480 | tf_op jit(solution)/shard_map/ppermute | solution.py:42
  137.7 18.8 %collective-permute-start.13 = (bf16[192,1536]{1,0:T(8,128)(2,1)S(1)}, bf16[192,1536]{1,0:T(8,128)(2,1)S(1)}, u32[]{:S(2)}, u32[]{:S(2)}) collective-permute-start(bf16[192,1536]{1,0:T(8,128)(2,1)S(1)} %pad_maximum_fusion.2), channel_id=1, source_target_pairs={{1,0},{2,1},{3,2},{0,3},{5,4},{6,5},{7,6},{4,7},{9,8},{10,9},{11,1... | collective-permute-start | bytes 1769480 | tf_op jit(solution)/shard_map/ppermute | solution.py:42
  144.0 24.0 %collective-permute-start.18 = (bf16[192,1536]{1,0:T(8,128)(2,1)S(1)}, bf16[192,1536]{1,0:T(8,128)(2,1)S(1)}, u32[]{:S(2)}, u32[]{:S(2)}) collective-permute-start(bf16[192,1536]{1,0:T(8,128)(2,1)S(1)} %pad_maximum_fusion.3), channel_id=1, source_target_pairs={{3,0},{0,1},{1,2},{2,3},{7,4},{4,5},{5,6},{6,7},{11,8},{8,9},{9,10... | collective-permute-start | bytes 1769480 | tf_op jit(solution)/shard_map/ppermute | solution.py:42
  144.2 23.9 %collective-permute-start.20 = (bf16[192,1536]{1,0:T(8,128)(2,1)S(1)}, bf16[192,1536]{1,0:T(8,128)(2,1)S(1)}, u32[]{:S(2)}, u32[]{:S(2)}) collective-permute-start(bf16[192,1536]{1,0:T(8,128)(2,1)S(1)} %pad_maximum_fusion.4), channel_id=1, source_target_pairs={{1,0},{2,1},{3,2},{0,3},{5,4},{6,5},{7,6},{4,7},{9,8},{10,9},{11,1... | collective-permute-start | bytes 1769480 | tf_op jit(solution)/shard_map/ppermute | solution.py:42
  156.7 15.9 %collective-permute-start.14 = (bf16[48,1536]{1,0:T(8,128)(2,1)S(1)}, bf16[48,1536]{1,0:T(8,128)(2,1)S(1)}, u32[]{:S(2)}, u32[]{:S(2)}) collective-permute-start(bf16[48,1536]{1,0:T(8,128)(2,1)S(1)} %get-tuple-element.31), channel_id=1, source_target_pairs={{12,0},{13,1},{14,2},{15,3},{0,4},{1,5},{2,6},{3,7},{4,8},{5,9},{6... | collective-permute-start | bytes 442376 | tf_op jit(solution)/shard_map/ppermute | solution.py:42
  159.3 18.9 %collective-permute-start.15 = (bf16[48,1536]{1,0:T(8,128)(2,1)S(1)}, bf16[48,1536]{1,0:T(8,128)(2,1)S(1)}, u32[]{:S(2)}, u32[]{:S(2)}) collective-permute-start(bf16[48,1536]{1,0:T(8,128)(2,1)S(1)} %get-tuple-element.33), channel_id=1, source_target_pairs={{4,0},{5,1},{6,2},{7,3},{8,4},{9,5},{10,6},{11,7},{12,8},{13,9},{1... | collective-permute-start | bytes 442376 | tf_op jit(solution)/shard_map/ppermute | solution.py:42
  161.0 17.3 %collective-permute-start.16 = (bf16[48,1536]{1,0:T(8,128)(2,1)S(1)}, bf16[48,1536]{1,0:T(8,128)(2,1)S(1)}, u32[]{:S(2)}, u32[]{:S(2)}) collective-permute-start(bf16[48,1536]{1,0:T(8,128)(2,1)S(1)} %get-tuple-element.32), channel_id=1, source_target_pairs={{8,0},{9,1},{10,2},{11,3},{12,4},{13,5},{14,6},{15,7},{0,8},{1,9},... | collective-permute-start | bytes 442376 | tf_op jit(solution)/shard_map/ppermute | solution.py:42
  168.3 10.0 %collective-permute-start.21 = (bf16[48,1536]{1,0:T(8,128)(2,1)S(1)}, bf16[48,1536]{1,0:T(8,128)(2,1)S(1)}, u32[]{:S(2)}, u32[]{:S(2)}) collective-permute-start(bf16[48,1536]{1,0:T(8,128)(2,1)S(1)} %get-tuple-element.36), channel_id=1, source_target_pairs={{12,0},{13,1},{14,2},{15,3},{0,4},{1,5},{2,6},{3,7},{4,8},{5,9},{6... | collective-permute-start | bytes 442376 | tf_op jit(solution)/shard_map/ppermute | solution.py:42
  170.9 16.9 %collective-permute-start.22 = (bf16[48,1536]{1,0:T(8,128)(2,1)S(1)}, bf16[48,1536]{1,0:T(8,128)(2,1)S(1)}, u32[]{:S(2)}, u32[]{:S(2)}) collective-permute-start(bf16[48,1536]{1,0:T(8,128)(2,1)S(1)} %get-tuple-element.38), channel_id=1, source_target_pairs={{4,0},{5,1},{6,2},{7,3},{8,4},{9,5},{10,6},{11,7},{12,8},{13,9},{1... | collective-permute-start | bytes 442376 | tf_op jit(solution)/shard_map/ppermute | solution.py:42
  172.6 15.2 %collective-permute-start.23 = (bf16[48,1536]{1,0:T(8,128)(2,1)S(1)}, bf16[48,1536]{1,0:T(8,128)(2,1)S(1)}, u32[]{:S(2)}, u32[]{:S(2)}) collective-permute-start(bf16[48,1536]{1,0:T(8,128)(2,1)S(1)} %get-tuple-element.37), channel_id=1, source_target_pairs={{8,0},{9,1},{10,2},{11,3},{12,4},{13,5},{14,6},{15,7},{0,8},{1,9},... | collective-permute-start | bytes 442376 | tf_op jit(solution)/shard_map/ppermute | solution.py:42
  189.2 12.0 %copy-start.19 = (bf16[64,3072]{1,0:T(8,128)(2,1)S(1)}, bf16[64,3072]{1,0:T(8,128)(2,1)}, u32[]{:S(2)}) copy-start(bf16[64,3072]{1,0:T(8,128)(2,1)} %param.16) | copy-start | bytes 1179652
  190.3 10.9 %copy-start.16 = (f32[64,3072]{1,0:T(8,128)S(1)}, f32[64,3072]{1,0:T(8,128)}, u32[]{:S(2)}) copy-start(f32[64,3072]{1,0:T(8,128)} %param.15) | copy-start | bytes 2359300
  190.3 10.9 %copy-start.17 = (f32[64,3072]{1,0:T(8,128)S(1)}, f32[64,3072]{1,0:T(8,128)}, u32[]{:S(2)}) copy-start(f32[64,3072]{1,0:T(8,128)} %param.17) | copy-start | bytes 2359300
  190.3 10.9 %copy-start.18 = (bf16[128,3072]{1,0:T(8,128)(2,1)S(1)}, bf16[128,3072]{1,0:T(8,128)(2,1)}, u32[]{:S(2)}) copy-start(bf16[128,3072]{1,0:T(8,128)(2,1)} %reduce-scatter.2.cloned.1.call-done) | copy-start | bytes 2359300
  190.3 10.9 %collective-permute-start.24 = (bf16[64,3072]{1,0:T(8,128)(2,1)S(1)}, bf16[64,3072]{1,0:T(8,128)(2,1)S(1)}, u32[]{:S(2)}, u32[]{:S(2)}) collective-permute-start(bf16[64,3072]{1,0:T(8,128)(2,1)S(1)} %dynamic-slice_bitcast_fusion.1), channel_id=1, source_target_pairs={{32,0},{48,16},{0,32},{16,48},{96,64},{112,80},{64,96},{80,112},{1... | collective-permute-start | bytes 1179656 | tf_op jit(solution)/shard_map/ppermute | solution.py:37
  201.2 1.8 copy-start.1
  (2 other events, 1.6 us)
Sparse Core Ops, SparseCore 0:
  9.9 63.6 all-gather.2
  75.4 44.4 all-gather.4
  122.5 40.5 reduce-scatter.1
where the time goes:
time: 211 us; the launch traced here: 210 us
  waiting for transfers between devices  92.4 us (44%)
  starting transfers between devices  56.2 us (27%)
  local copies, waits for them, and re-layouts  21 us (10%)
  between operations  14.2 us (7%)
  Pallas kernels  13.1 us (6%)
  other arithmetic  12.1 us (6%)
    ppermute x23, waiting for transfers between devices, get_tensor(): return lax.ppermute(value, 'tensor', pairs)  70.6 us
    ppermute x23, starting transfers between devices, get_tensor(): return lax.ppermute(value, 'tensor', pairs)  54.1 us
    unnamed x48, local copies, waits for them, and re-layouts  13.3 us
    all_gather x1, waiting for transfers between devices, local(): down = lax.all_gather(w_down, 'dp', axis=0, tiled=True)  12.6 us
    ppermute x2, waiting for transfers between devices, get_dp(): return lax.ppermute(value, 'dp', pairs)  7.82 us
    pallas_call x1, Pallas kernels, up_call(): pl.pallas_call(up_kernel, out_shape=jax.ShapeDtypeStruct((768, 1024), jnp...  6.72 us
    pallas_call x2, Pallas kernels, down_call(): pl.pallas_call(down_kernel, out_shape=[jax.ShapeDtypeStruct((192, 2 * wid...  6.38 us
    convert_element_type x1, other arithmetic, local(): total([keep, get_dp(give, c=1)]).astype(jnp.bfloat16).reshape(512, D)  5.73 us
  transfers between devices with their start and end apart: 28, of which 14 were waited for; matrix products, arithmetic and copies ran while one was open for 10% of the time, Pallas kernels for 6%

commit v1 on v0

--- a/solution.py
+++ b/solution.py
@@ -78,55 +78,135 @@
     return 0.5 * u * (1.0 + lax.erf(u * 0.7071067811865476))
 
 
-def up_kernel(y0, y1, y3, y2_left, y2_right, w, h):
-    def put(at, u):
-        h[at * 192 : (at + 1) * 192, :] = gelu(u).astype(jnp.bfloat16)
-
-    for at, y in ((0, y0), (1, y1), (3, y3)):
-        put(at, jnp.dot(y[...], w[...], preferred_element_type=jnp.float32))
-    u = jnp.dot(y2_left[...], w[: D // 2], preferred_element_type=jnp.float32)
-    put(2, u + jnp.dot(y2_right[...], w[D // 2 :], preferred_element_type=jnp.float32))
+def prep_kernel(routes, tokens, rows):
+    routed = jnp.where((routes[0:1, :] == 0) | (routes[1:2, :] == 0), 1.0, 0.0)
+    before = lax.broadcasted_iota(jnp.int32, (128, 128), 0) < lax.broadcasted_iota(jnp.int32, (128, 128), 1)
+    slot = jnp.dot(routed, jnp.where(before, 1.0, 0.0), preferred_element_type=jnp.float32)
+    wanted = lax.broadcasted_iota(jnp.int32, (CAP, 128), 0).astype(jnp.float32)
+    picks = jnp.where((wanted == slot) & (routed > 0.5), 1.0, 0.0).astype(jnp.bfloat16)
+    for n in range(N_X):
+        block = jnp.dot(picks, tokens[:, n * 768 : (n + 1) * 768], preferred_element_type=jnp.float32)
+        block = block.astype(jnp.bfloat16)
+        cut = [block[:, k * 192 : (k + 1) * 192] for k in (0, 2, 1, 3)]
+        rows[:, n * 768 : (n + 1) * 768] = jnp.concatenate(cut, axis=1)
+
+
+def prep_call(routes, tokens):
+    return pl.pallas_call(
+        prep_kernel,
+        out_shape=jax.ShapeDtypeStruct((CAP, D), jnp.bfloat16),
+        in_specs=[pl.BlockSpec(memory_space=pltpu.VMEM)] * 2,
+        out_specs=pl.BlockSpec(memory_space=pltpu.VMEM),
+        compiler_params=pltpu.CompilerParams(vmem_limit_bytes=16 << 20),
+        name="prep",
+    )(routes, tokens)
+
+
+def finish_kernel(routes, gating, *refs):
+    parts, out = refs[:8], refs[8]
+    routed = jnp.where((routes[:, 0:1] == 0) | (routes[:, 1:2] == 0), 1.0, 0.0)
+    before = lax.broadcasted_iota(jnp.int32, (128, 128), 1) < lax.broadcasted_iota(jnp.int32, (128, 128), 0)
+    slot = jnp.dot(jnp.where(before, 1.0, 0.0), routed, preferred_element_type=jnp.float32)
+    wanted = lax.broadcasted_iota(jnp.int32, (128, CAP), 1).astype(jnp.float32)
+    picks = jnp.where((wanted == slot) & (routed > 0.5), 1.0, 0.0).astype(jnp.bfloat16)
+    for side in range(2):
+        owned = total([p[...] for p in parts[4 * side : 4 * side + 4]])
+        high = owned.astype(jnp.bfloat16)
+        low = (owned - high.astype(jnp.float32)).astype(jnp.bfloat16)
+        taken = jnp.dot(picks, high, preferred_element_type=jnp.float32)
+        taken = taken + jnp.dot(picks, low, preferred_element_type=jnp.float32)
+        at = side * (D // 2)
+        out[:, at : at + D // 2] = (taken * gating[...]).astype(jnp.bfloat16)
+
+
+def finish_call(routes, gating, parts):
+    return pl.pallas_call(
+        finish_kernel,
+        out_shape=jax.ShapeDtypeStruct((128, D), jnp.bfloat16),
+        in_specs=[pl.BlockSpec(memory_space=pltpu.VMEM)] * 10,
+        out_specs=pl.BlockSpec(memory_space=pltpu.VMEM),
+        compiler_params=pltpu.CompilerParams(vmem_limit_bytes=16 << 20),
+        name="finish",
+    )(routes, gating, *parts)
+
+
+def put_hidden(h, at, n, u):
+    act = gelu(u).astype(jnp.bfloat16)
+    cut = [act[:, k * 64 : (k + 1) * 64] for k in (0, 2, 1, 3)]
+    h[at * 192 : (at + 1) * 192, n * 256 : (n + 1) * 256] = jnp.concatenate(cut, axis=1)
+
+
+def up_kernel(*refs):
+    *rows, w, h, held, sems = refs
+    copies = [
+        pltpu.make_async_copy(w.at[:, n * 256 : (n + 1) * 256], held.at[n], sems.at[n]) for n in range(N_X)
+    ]
+    for copy in copies:
+        copy.start()
+    for n in range(N_X):
+        copies[n].wait()
+        for at, y in enumerate(rows):
+            put_hidden(h, at, n, jnp.dot(y[...], held[n], preferred_element_type=jnp.float32))
+
+
+def up_halves_kernel(left, right, w, h, held, sems):
+    copies = [
+        pltpu.make_async_copy(w.at[n * 768 : (n + 1) * 768, :], held.at[n], sems.at[n]) for n in range(4)
+    ]
+    for copy in copies:
+        copy.start()
+    u = None
+    for n in range(4):
+        copies[n].wait()
+        part = (left, right)[n // 2][:, (n % 2) * 768 : (n % 2 + 1) * 768]
+        term = jnp.dot(part, held[n], preferred_element_type=jnp.float32)
+        u = term if u is None else u + term
+    for n in range(N_X):
+        put_hidden(h, 0, n, u[:, n * 256 : (n + 1) * 256])
 
 
 def up_call(rows, w):
-    whole = lambda shape: pl.BlockSpec(shape, lambda n: (0, 0))
+    count = sum(r.shape[0] * r.shape[1] for r in rows) // D
+    halves = rows[0].shape[1] < D
+    vmem = pl.BlockSpec(memory_space=pltpu.VMEM)
     return pl.pallas_call(
-        up_kernel,
-        out_shape=jax.ShapeDtypeStruct((768, 1024), jnp.bfloat16),
-        grid=(4,),
-        in_specs=[whole(r.shape) for r in rows] + [pl.BlockSpec((D, 256), lambda n: (0, n))],
-        out_specs=pl.BlockSpec((768, 256), lambda n: (0, n)),
-        compiler_params=pltpu.CompilerParams(vmem_limit_bytes=VMEM),
+        up_halves_kernel if halves else up_kernel,
+        out_shape=jax.ShapeDtypeStruct((count, 1024), jnp.bfloat16),
+        in_specs=[vmem] * len(rows) + [pl.BlockSpec(memory_space=pltpu.HBM)],
+        out_specs=vmem,
+        scratch_shapes=[pltpu.VMEM((4, 768, 1024) if halves else (N_X, D, 256), jnp.bfloat16), pltpu.SemaphoreType.DMA((N_X,))],
+        compiler_params=pltpu.CompilerParams(vmem_limit_bytes=12 << 20),
         cost_estimate=pl.CostEstimate(
-            flops=2 * 768 * 1024 * D, bytes_accessed=2 * (768 * D + D * 1024 + 768 * 1024), transcendentals=0
+            flops=2 * count * 1024 * D, bytes_accessed=2 * (count * D + D * 1024 + count * 1024), transcendentals=0
         ),
         name="up",
     )(*rows, w)
 
 
-def down_kernel(h, d, p0, p1, p2, p3):
-    for at, p in ((2, p2), (1, p1), (3, p3), (0, p0)):
+def down_kernel(h_near, h_far, d, p0, p1, p2, p3):
+    for h, at, p in ((h_far, 0, p2), (h_near, 1, p1), (h_near, 2, p3), (h_near, 0, p0)):
         rows = h[at * 192 : (at + 1) * 192, :]
         p[...] = jnp.dot(rows, d[...], preferred_element_type=jnp.float32).astype(jnp.bfloat16)
 
 
-def down_call(h, d, first, width):
+def down_call(h_near, h_far, d, first, width):
     at = first // width
     return pl.pallas_call(
         down_kernel,
         out_shape=[jax.ShapeDtypeStruct((192, 2 * width), jnp.bfloat16)] * 4,
         grid=(2,),
         in_specs=[
-            pl.BlockSpec((768, 1024), lambda n: (0, 0)),
+            pl.BlockSpec((576, 1024), lambda n: (0, 0)),
+            pl.BlockSpec((192, 1024), lambda n: (0, 0)),
             pl.BlockSpec((1024, width), lambda n: (0, n + at)),
         ],
         out_specs=[pl.BlockSpec((192, width), lambda n: (0, n))] * 4,
-        compiler_params=pltpu.CompilerParams(vmem_limit_bytes=VMEM),
+        compiler_params=pltpu.CompilerParams(vmem_limit_bytes=20 << 20),
         cost_estimate=pl.CostEstimate(
             flops=2 * 768 * 1024 * 2 * width, bytes_accessed=2 * (768 * 1024 + 1792 * 2 * width), transcendentals=0
         ),
         name="down",
-    )(h, d)
+    )(h_near, h_far, d)
 
 
 def split_sum(parts, send):
@@ -144,52 +224,56 @@
 
 def local(tokens, routes, router, w_up, w_down, grad_parts, master, moment_one, moment_two):
     here = lax.axis_index("dp")
-    x, zl, c = here // 4, (here // 2) % 2, here % 2
+    zl = (here // 2) % 2
     half = D // 2
-
-    up = lax.all_gather(w_up, "dp", axis=0, tiled=True)
-    down = lax.all_gather(w_down, "dp", axis=0, tiled=True)
+    tie = lax.optimization_barrier
+    groups = [[dp_of(i, j, k) for i in range(N_X) for k in range(N_C)] for j in range(N_ZL)]
+
+    def gathered(value):
+        came = get_dp(value, zl=1)
+        pair = jnp.concatenate([jnp.where(zl == 0, value, came), jnp.where(zl == 0, came, value)], axis=0)
+        return lax.all_gather(pair, "dp", axis=0, tiled=True, axis_index_groups=groups)
+
+    up = gathered(w_up)
 
     routed, gating = gating_of(tokens, routes, router)
-    slot_index = jnp.cumsum(routed.astype(jnp.int32)) - 1
-    slot_iota = jnp.arange(CAP, dtype=jnp.int32)
-    picks = ((slot_index[None, :] == slot_iota[:, None]) & routed[None, :]).astype(jnp.bfloat16)
-    own = jnp.dot(picks, tokens, preferred_element_type=jnp.float32).astype(jnp.bfloat16)
+    own = prep_call(routes.T, tokens)
     near = [get_tensor(own, y=k) for k in (1, 3)]
     far = jnp.concatenate([get_tensor(own, zh=k) for k in (1, 3, 2)], axis=0)
+    near[0], near[1], w_down = tie((near[0], near[1], w_down))
+    far, near[0], near[1] = tie((far, near[0], near[1]))
+    down = gathered(w_down)
     y0 = jnp.concatenate([own, far], axis=0)
     y1 = jnp.concatenate([near[0], get_tensor(far, y=1)], axis=0)
     y3 = jnp.concatenate([near[1], get_tensor(far, y=3)], axis=0)
+    y0, y1, y3, up = tie((y0, y1, y3, up))
     y2_left = get_tensor(y1[:, :half], y=1)
     y2_right = get_tensor(y3[:, half:], y=3)
 
-    grads = grad_parts[0].reshape(8, 2, 64, D)
-    keep = lax.dynamic_index_in_dim(grads, c, axis=1, keepdims=False)
-    give = lax.dynamic_index_in_dim(grads, 1 - c, axis=1, keepdims=False)
-    give, far_seen = lax.optimization_barrier((give, far))
-    core_sum = total([keep, get_dp(give, c=1)]).astype(jnp.bfloat16).reshape(512, D)
-    hidden = up_call((y0, y1, y3, y2_left, y2_right), up)
-    core_sum, hidden = lax.optimization_barrier((core_sum, hidden))
-    xgroups = [[dp_of(i, j, k) for i in range(N_X)] for j in range(N_ZL) for k in range(N_C)]
+    grads, _ = tie((grad_parts[0], far))
+    grads = grads.reshape(N_X, N_ZL, N_C, 64, D).transpose(0, 2, 1, 3, 4).reshape(1024, D)
+
+    h_near = up_call((y0, y1, y3), up)
+    y2_left, y2_right, h_near = tie((y2_left, y2_right, h_near))
+    h_far = up_call((y2_left, y2_right), up)
+    grads, h_far = tie((grads, h_far))
     x_sum = lax.psum_scatter(
-        core_sum, "dp", scatter_dimension=0, tiled=True, axis_index_groups=xgroups
+        grads, "dp", scatter_dimension=0, tiled=True, axis_index_groups=groups
     ).reshape(2, 64, D)
 
     send_y = lambda value, k: get_tensor(value, y=-k)
     owned = []
     for first in (0, half):
-        ysum = split_sum(down_call(hidden, down, first, half // 2), send_y)
+        ysum = split_sum(down_call(h_near, h_far, down, first, half // 2), send_y)
         ysum = lax.optimization_barrier(ysum.astype(jnp.bfloat16)).reshape(4, CAP, half)
         came = [ysum[0]] + [get_tensor(ysum[i], zh=-k) for i, k in ((1, 1), (2, 3), (3, 2))]
-        owned.append(total(came))
-    owned = jnp.concatenate(owned, axis=1)
-    combined = jnp.take(owned, jnp.clip(slot_index, 0, CAP - 1), axis=0)
-    mixed = (combined * gating[:, None]).astype(jnp.bfloat16)
-
+        owned += came
     keep = lax.dynamic_index_in_dim(x_sum, zl, axis=0, keepdims=False)
     give = lax.dynamic_index_in_dim(x_sum, 1 - zl, axis=0, keepdims=False)
     grad_total = total([keep, get_dp(give, zl=1)])
     new_master, new_one, new_two = adam_step(grad_total, master, moment_one, moment_two)
+    owned[-1], new_master, new_one, new_two = tie((owned[-1], new_master, new_one, new_two))
+    mixed = finish_call(routes, gating[:, None], owned)
     return (mixed, new_master, new_one, new_two)
 
 

time: 211 us -> 200 us (0.948)
  local copies, waits for them, and re-layouts: 21 us -> 12.4 us
  Pallas kernels: 13.1 us -> 17.8 us
  other arithmetic: 12.1 us -> 7.94 us
    ppermute x2 -> x3, waiting for transfers between devices: 7.82 us -> 28.7 us  [get_dp(): return lax.ppermute(value, 'dp', pairs)]
    all_gather x2, waiting for transfers between devices: 12.6 us -> 0.29 us  [gathered(): lax.all_gather(pair, 'dp', axis=0, tiled=True, axis_index_groups=groups)]
    unnamed x48 -> x31, local copies, waits for them, and re-layouts: 13.3 us -> 3.36 us
    ppermute x23, waiting for transfers between devices: 70.6 us -> 61.4 us  [get_tensor(): return lax.ppermute(value, 'tensor', pairs)]
    convert_element_type x2 -> x0, other arithmetic: 6.83 us -> none  [the longest x1 5.73 us: local(): total([keep, get_dp(give, c=1)]).astype(jnp.bfloat16).reshape(512, D)]
    transpose x0 -> x1, local copies, waits for them, and re-layouts: none -> 6.38 us  [local(): grads.reshape(N_X, N_ZL, N_C, 64, D).transpose(0, 2, 1, 3, 4)]
    pallas_call x1 -> x4, Pallas kernels: 6.72 us -> 11.3 us  [the longest x2 9.13 us: up_call(): pl.pallas_call(up_halves_kernel if halves else up_kernel, out_shape=jax.S...]
    ppermute x23, starting transfers between devices: 54.1 us -> 49.7 us  [get_tensor(): return lax.ppermute(value, 'tensor', pairs)]
  transfers between devices with their start and end apart: 28 -> 29, of which waited for: 14 -> 15; matrix products, arithmetic and copies ran while one was open for 10% -> 8% of each run, Pallas kernels for 6% -> 8%
where the time goes in v1:
time: 200 us; the launch traced here: 198 us
  waiting for transfers between devices  90.4 us (45%)
  starting transfers between devices  55.4 us (28%)
  Pallas kernels  17.8 us (9%)
  between operations  14.2 us (7%)
  local copies, waits for them, and re-layouts  12.4 us (6%)
  other arithmetic  7.94 us (4%)
    ppermute x23, waiting for transfers between devices, get_tensor(): return lax.ppermute(value, 'tensor', pairs)  61.4 us
    ppermute x23, starting transfers between devices, get_tensor(): return lax.ppermute(value, 'tensor', pairs)  49.7 us
    ppermute x3, waiting for transfers between devices, get_dp(): return lax.ppermute(value, 'dp', pairs)  28.7 us
    pallas_call x2, Pallas kernels, up_call(): pl.pallas_call(up_halves_kernel if halves else up_kernel, out_shape=jax.S...  9.13 us
    pallas_call x2, Pallas kernels, down_call(): pl.pallas_call(down_kernel, out_shape=[jax.ShapeDtypeStruct((192, 2 * wid...  6.5 us
    transpose x1, local copies, waits for them, and re-layouts, local(): grads.reshape(N_X, N_ZL, N_C, 64, D).transpose(0, 2, 1, 3, 4)  6.38 us
    ppermute x3, starting transfers between devices, get_dp(): return lax.ppermute(value, 'dp', pairs)  5.55 us
  transfers between devices with their start and end apart: 29, of which 15 were waited for; matrix products, arithmetic and copies ran while one was open for 8% of the time, Pallas kernels for 8%

profile of v1, /device:TPU:2, one launch (start us, length us, event | category | flops | bytes accessed | tf_op | source)
XLA Modules:
  0.0 198.5 jit_solution(13407582381306076983)
XLA Ops:
  7.2 2.0 %collective-permute-start.7 = (bf16[192,1024]{1,0:T(8,128)(2,1)}, bf16[192,1024]{1,0:T(8,128)(2,1)S(1)}, u32[]{:S(2)}, u32[]{:S(2)}) collective-permute-start(bf16[192,1024]{1,0:T(8,128)(2,1)} %param.12), channel_id=1, source_target_pairs={{32,0},{48,16},{0,32},{16,48},{96,64},{112,80},{64,96},{80,112},{1... | collective-permute-start | bytes 1179656 | tf_op jit(solution)/shard_map/ppermute | solution.py:37
  9.2 9.3 %collective-permute-done.7 = bf16[192,1024]{1,0:T(8,128)(2,1)S(1)} collective-permute-done((bf16[192,1024]{1,0:T(8,128)(2,1)}, bf16[192,1024]{1,0:T(8,128)(2,1)S(1)}, u32[]{:S(2)}, u32[]{:S(2)}) %collective-permute-start.7) | collective-permute-done | bytes 393248 | tf_op jit(solution)/shard_map/ppermute | solution.py:37
  18.6 1.1 broadcast_select_fusion.3
  19.6 0.9 pad_maximum_fusion.4
  21.0 0.4 prep.1
  21.5 3.1 %collective-permute-start.3 = (bf16[48,3072]{1,0:T(8,128)(2,1)S(1)}, bf16[48,3072]{1,0:T(8,128)(2,1)S(1)}, u32[]{:S(2)}, u32[]{:S(2)}) collective-permute-start(bf16[48,3072]{1,0:T(8,128)(2,1)S(1)} %prep.1), channel_id=1, source_target_pairs={{1,0},{2,1},{3,2},{0,3},{5,4},{6,5},{7,6},{4,7},{9,8},{10,9},{11,1... | collective-permute-start | bytes 884744 | tf_op jit(solution)/shard_map/ppermute | solution.py:42
  24.6 5.6 %collective-permute-done.3 = bf16[48,3072]{1,0:T(8,128)(2,1)S(1)} collective-permute-done((bf16[48,3072]{1,0:T(8,128)(2,1)S(1)}, bf16[48,3072]{1,0:T(8,128)(2,1)S(1)}, u32[]{:S(2)}, u32[]{:S(2)}) %collective-permute-start.3) | collective-permute-done | bytes 294944 | tf_op jit(solution)/shard_map/ppermute | solution.py:42
  30.2 3.4 %collective-permute-done.4 = bf16[48,3072]{1,0:T(8,128)(2,1)S(1)} collective-permute-done((bf16[48,3072]{1,0:T(8,128)(2,1)S(1)}, bf16[48,3072]{1,0:T(8,128)(2,1)S(1)}, u32[]{:S(2)}, u32[]{:S(2)}) %collective-permute-start.4) | collective-permute-done | bytes 294944 | tf_op jit(solution)/shard_map/ppermute | solution.py:42
  33.6 1.5 collective-permute-start.10
  35.1 7.4 %collective-permute-done.10 = bf16[64,3072]{1,0:T(8,128)(2,1)S(1)} collective-permute-done((bf16[64,3072]{1,0:T(8,128)(2,1)S(1)}, bf16[64,3072]{1,0:T(8,128)(2,1)S(1)}, u32[]{:S(2)}, u32[]{:S(2)}) %collective-permute-start.10) | collective-permute-done | bytes 393248 | tf_op jit(solution)/shard_map/ppermute | solution.py:37
  42.6 0.9 pad_maximum_fusion.5
  43.6 5.8 %collective-permute-start = (bf16[48,3072]{1,0:T(8,128)(2,1)S(1)}, bf16[48,3072]{1,0:T(8,128)(2,1)S(1)}, u32[]{:S(2)}, u32[]{:S(2)}) collective-permute-start(bf16[48,3072]{1,0:T(8,128)(2,1)S(1)} %prep.1), channel_id=1, source_target_pairs={{4,0},{5,1},{6,2},{7,3},{8,4},{9,5},{10,6},{11,7},{12,8},{13,9},{1... | collective-permute-start | bytes 884744 | tf_op jit(solution)/shard_map/ppermute | solution.py:42
  49.4 3.8 %collective-permute-start.2 = (bf16[48,3072]{1,0:T(8,128)(2,1)S(1)}, bf16[48,3072]{1,0:T(8,128)(2,1)S(1)}, u32[]{:S(2)}, u32[]{:S(2)}) collective-permute-start(bf16[48,3072]{1,0:T(8,128)(2,1)S(1)} %prep.1), channel_id=1, source_target_pairs={{8,0},{9,1},{10,2},{11,3},{12,4},{13,5},{14,6},{15,7},{0,8},{1,9},... | collective-permute-start | bytes 884744 | tf_op jit(solution)/shard_map/ppermute | solution.py:42
  53.2 18.6 %collective-permute-done = bf16[48,3072]{1,0:T(8,128)(2,1)S(1)} collective-permute-done((bf16[48,3072]{1,0:T(8,128)(2,1)S(1)}, bf16[48,3072]{1,0:T(8,128)(2,1)S(1)}, u32[]{:S(2)}, u32[]{:S(2)}) %collective-permute-start) | collective-permute-done | bytes 294944 | tf_op jit(solution)/shard_map/ppermute | solution.py:42
  72.5 3.2 %collective-permute-start.5 = (bf16[144,3072]{1,0:T(8,128)(2,1)S(1)}, bf16[144,3072]{1,0:T(8,128)(2,1)S(1)}, u32[]{:S(2)}, u32[]{:S(2)}) collective-permute-start(bf16[144,3072]{1,0:T(8,128)(2,1)S(1)} %pad_maximum_fusion.3), channel_id=1, source_target_pairs={{1,0},{2,1},{3,2},{0,3},{5,4},{6,5},{7,6},{4,7},{9,8},{10,9},{11,1... | collective-permute-start | bytes 2654216 | tf_op jit(solution)/shard_map/ppermute | solution.py:42
  75.8 1.1 pad_maximum_fusion.refs_0_
  76.9 12.0 %collective-permute-done.6 = bf16[144,3072]{1,0:T(8,128)(2,1)S(1)} collective-permute-done((bf16[144,3072]{1,0:T(8,128)(2,1)S(1)}, bf16[144,3072]{1,0:T(8,128)(2,1)S(1)}, u32[]{:S(2)}, u32[]{:S(2)}) %collective-permute-start.6) | collective-permute-done | bytes 884768 | tf_op jit(solution)/shard_map/ppermute | solution.py:42
  89.0 3.2 %collective-permute-done.5 = bf16[144,3072]{1,0:T(8,128)(2,1)S(1)} collective-permute-done((bf16[144,3072]{1,0:T(8,128)(2,1)S(1)}, bf16[144,3072]{1,0:T(8,128)(2,1)S(1)}, u32[]{:S(2)}, u32[]{:S(2)}) %collective-permute-start.5) | collective-permute-done | bytes 884768 | tf_op jit(solution)/shard_map/ppermute | solution.py:42
  92.3 2.4 %collective-permute-start.8 = (bf16[192,1536]{1,0:T(8,128)(2,1)S(1)}, bf16[192,1536]{1,0:T(8,128)(2,1)S(1)}, u32[]{:S(2)}, u32[]{:S(2)}) collective-permute-start(bf16[192,1536]{1,0:T(8,128)(2,1)S(1)} %slice.92), channel_id=1, source_target_pairs={{1,0},{2,1},{3,2},{0,3},{5,4},{6,5},{7,6},{4,7},{9,8},{10,9},{11,1... | collective-permute-start | bytes 1769480 | tf_op jit(solution)/shard_map/ppermute | solution.py:42
  95.1 6.4 %copy.43 = bf16[4,2,2,64,3072]{4,3,2,1,0:T(8,128)(2,1)} copy(bf16[4,2,2,64,3072]{4,3,1,2,0:T(8,128)(2,1)} %bitcast.21) | data formatting | bytes 12582912 | tf_op jit(solution)/shard_map/transpose | solution.py:254
  101.5 6.9 %up.2.h_near = bf16[576,1024]{1,0:T(8,128)(2,1)S(1)} custom-call(bf16[192,3072]{1,0:T(8,128)(2,1)S(1)} %copy-done.2, bf16[192,3072]{1,0:T(8,128)(2,1)S(1)} %pad_maximum_fusion.1.refs_1_, bf16[192,3072]{1,0:T(8,128)(2,1)S(1)} %pad_maximum_fusion.2.refs_2_, bf16[3072,1024]{1,0:T(8,128)(2,1)S(1)} %bitcast.18), custom_call_target="tpu_custom_call" | custom-call | flops 3623878656 | bytes 11010048 | tf_op jit(solution)/shard_map/up/pallas_call | solution.py:172
  108.5 2.2 %up.3.h_far = bf16[192,1024]{1,0:T(8,128)(2,1)S(1)} custom-call(bf16[192,1536]{1,0:T(8,128)(2,1)S(1)} %collective-permute-done.8.left, bf16[192,1536]{1,0:T(8,128)(2,1)S(1)} %collective-permute-done.9.right, bf16[3072,1024]{1,0:T(8,128)(2,1)S(1)} %bitcast.18), custom_call_target="tpu_custom_call" | custom-call | flops 1207959552 | bytes 7864320 | tf_op jit(solution)/shard_map/up/pallas_call | solution.py:172
  112.1 2.8 %copy-done.4 = bf16[1024,3072]{1,0:T(8,128)(2,1)S(1)} copy-done((bf16[1024,3072]{1,0:T(8,128)(2,1)S(1)}, bf16[1024,3072]{1,0:T(8,128)(2,1)}, u32[]{:S(2)}) %copy-start.4) | copy-done | bytes 6291480
  114.8 3.3 %down.3 = (bf16[192,1536]{1,0:T(8,128)(2,1)S(1)}, bf16[192,1536]{1,0:T(8,128)(2,1)S(1)}, bf16[192,1536]{1,0:T(8,128)(2,1)S(1)}, bf16[192,1536]{1,0:T(8,128)(2,1)S(1)}) custom-call(bf16[576,1024]{1,0:T(8,128)(2,1)S(1)} %copy-done.6, bf16[192,1024]{1,0:T(8,128)(2,1)S(1)} %up.3.h_far, bf16[1024,3072]{1,0:T(8,128)(2,1)S(1)} %copy-done.4), custom_call_target="tpu_custom_call" | custom-call | flops 2415919104 | bytes 7077888 | tf_op jit(solution)/shard_map/down/pallas_call | solution.py:194
  118.2 1.6 collective-permute-start.18
  119.7 1.8 collective-permute-start.20
  121.6 3.2 %down.2 = (bf16[192,1536]{1,0:T(8,128)(2,1)S(1)}, bf16[192,1536]{1,0:T(8,128)(2,1)S(1)}, bf16[192,1536]{1,0:T(8,128)(2,1)S(1)}, bf16[192,1536]{1,0:T(8,128)(2,1)S(1)}) custom-call(bf16[576,1024]{1,0:T(8,128)(2,1)S(1)} %copy-done.6, bf16[192,1024]{1,0:T(8,128)(2,1)S(1)} %up.3.h_far, bf16[1024,3072]{1,0:T(8,128)(2,1)S(1)} %copy-done.4), custom_call_target="tpu_custom_call" | custom-call | flops 2415919104 | bytes 7077888 | tf_op jit(solution)/shard_map/down/pallas_call | solution.py:194
  124.9 0.6 collective-permute-start.11
  125.5 3.0 %collective-permute-start.13 = (bf16[192,768]{1,0:T(8,128)(2,1)S(1)}, bf16[192,768]{1,0:T(8,128)(2,1)S(1)}, u32[]{:S(2)}, u32[]{:S(2)}) collective-permute-start(bf16[192,768]{1,0:T(8,128)(2,1)S(1)} %get-tuple-element.78), channel_id=1, source_target_pairs={{1,0},{2,1},{3,2},{0,3},{5,4},{6,5},{7,6},{4,7},{9,8},{10,9},{11,1... | collective-permute-start | bytes 884744 | tf_op jit(solution)/shard_map/ppermute | solution.py:42
  128.7 1.0 collective-permute-start.19
  129.9 2.3 %collective-permute-start.21 = (bf16[192,1536]{1,0:T(8,128)(2,1)S(1)}, bf16[192,1536]{1,0:T(8,128)(2,1)S(1)}, u32[]{:S(2)}, u32[]{:S(2)}) collective-permute-start(bf16[192,1536]{1,0:T(8,128)(2,1)S(1)} %pad_maximum_fusion.9), channel_id=1, source_target_pairs={{1,0},{2,1},{3,2},{0,3},{5,4},{6,5},{7,6},{4,7},{9,8},{10,9},{11,1... | collective-permute-start | bytes 1769480 | tf_op jit(solution)/shard_map/ppermute | solution.py:42
  132.2 4.1 %collective-permute-done.11 = bf16[192,768]{1,0:T(8,128)(2,1)S(1)} collective-permute-done((bf16[192,768]{1,0:T(8,128)(2,1)S(1)}, bf16[192,768]{1,0:T(8,128)(2,1)S(1)}, u32[]{:S(2)}, u32[]{:S(2)}) %collective-permute-start.11) | collective-permute-done | bytes 294944 | tf_op jit(solution)/shard_map/ppermute | solution.py:42
  136.7 3.3 %collective-permute-start.14 = (bf16[192,1536]{1,0:T(8,128)(2,1)S(1)}, bf16[192,1536]{1,0:T(8,128)(2,1)S(1)}, u32[]{:S(2)}, u32[]{:S(2)}) collective-permute-start(bf16[192,1536]{1,0:T(8,128)(2,1)S(1)} %pad_maximum_fusion.7), channel_id=1, source_target_pairs={{1,0},{2,1},{3,2},{0,3},{5,4},{6,5},{7,6},{4,7},{9,8},{10,9},{11,1... | collective-permute-start | bytes 1769480 | tf_op jit(solution)/shard_map/ppermute | solution.py:42
  140.0 9.0 %collective-permute-done.19 = bf16[192,1536]{1,0:T(8,128)(2,1)S(1)} collective-permute-done((bf16[192,1536]{1,0:T(8,128)(2,1)S(1)}, bf16[192,1536]{1,0:T(8,128)(2,1)S(1)}, u32[]{:S(2)}, u32[]{:S(2)}) %collective-permute-start.19) | collective-permute-done | bytes 589856 | tf_op jit(solution)/shard_map/ppermute | solution.py:42
  149.2 0.8 fusion.2
  149.9 5.7 %collective-permute-start.24 = (bf16[48,1536]{1,0:T(8,128)(2,1)}, bf16[48,1536]{1,0:T(8,128)(2,1)S(1)}, u32[]{:S(2)}, u32[]{:S(2)}) collective-permute-start(bf16[48,1536]{1,0:T(8,128)(2,1)} %get-tuple-element.67), channel_id=1, source_target_pairs={{8,0},{9,1},{10,2},{11,3},{12,4},{13,5},{14,6},{15,7},{0,8},{1,9},... | collective-permute-start | bytes 442376 | tf_op jit(solution)/shard_map/ppermute | solution.py:42
  155.7 2.4 %collective-permute-start.22 = (bf16[48,1536]{1,0:T(8,128)(2,1)}, bf16[48,1536]{1,0:T(8,128)(2,1)S(1)}, u32[]{:S(2)}, u32[]{:S(2)}) collective-permute-start(bf16[48,1536]{1,0:T(8,128)(2,1)} %get-tuple-element.69), channel_id=1, source_target_pairs={{12,0},{13,1},{14,2},{15,3},{0,4},{1,5},{2,6},{3,7},{4,8},{5,9},{6... | collective-permute-start | bytes 442376 | tf_op jit(solution)/shard_map/ppermute | solution.py:42
  158.1 1.7 collective-permute-start.23
  159.8 0.5 collective-permute-done.12
  160.6 1.2 dynamic-slice_bitcast_fusion
  161.7 2.0 %collective-permute-start.25 = (bf16[64,3072]{1,0:T(8,128)(2,1)S(1)}, bf16[64,3072]{1,0:T(8,128)(2,1)S(1)}, u32[]{:S(2)}, u32[]{:S(2)}) collective-permute-start(bf16[64,3072]{1,0:T(8,128)(2,1)S(1)} %dynamic-slice_bitcast_fusion), channel_id=1, source_target_pairs={{32,0},{48,16},{0,32},{16,48},{96,64},{112,80},{64,96},{80,112},{1... | collective-permute-start | bytes 1179656 | tf_op jit(solution)/shard_map/ppermute | solution.py:37
  163.8 2.3 %collective-permute-start.15 = (bf16[48,1536]{1,0:T(8,128)(2,1)S(1)}, bf16[48,1536]{1,0:T(8,128)(2,1)S(1)}, u32[]{:S(2)}, u32[]{:S(2)}) collective-permute-start(bf16[48,1536]{1,0:T(8,128)(2,1)S(1)} %get-tuple-element.75), channel_id=1, source_target_pairs={{12,0},{13,1},{14,2},{15,3},{0,4},{1,5},{2,6},{3,7},{4,8},{5,9},{6... | collective-permute-start | bytes 442376 | tf_op jit(solution)/shard_map/ppermute | solution.py:42
  166.1 3.0 %collective-permute-start.16 = (bf16[48,1536]{1,0:T(8,128)(2,1)S(1)}, bf16[48,1536]{1,0:T(8,128)(2,1)S(1)}, u32[]{:S(2)}, u32[]{:S(2)}) collective-permute-start(bf16[48,1536]{1,0:T(8,128)(2,1)S(1)} %get-tuple-element.74), channel_id=1, source_target_pairs={{4,0},{5,1},{6,2},{7,3},{8,4},{9,5},{10,6},{11,7},{12,8},{13,9},{1... | collective-permute-start | bytes 442376 | tf_op jit(solution)/shard_map/ppermute | solution.py:42
  169.0 11.9 %collective-permute-done.25 = bf16[64,3072]{1,0:T(8,128)(2,1)S(1)} collective-permute-done((bf16[64,3072]{1,0:T(8,128)(2,1)S(1)}, bf16[64,3072]{1,0:T(8,128)(2,1)S(1)}, u32[]{:S(2)}, u32[]{:S(2)}) %collective-permute-start.25) | collective-permute-done | bytes 393248 | tf_op jit(solution)/shard_map/ppermute | solution.py:37
  181.0 2.1 %collective-permute-start.17 = (bf16[48,1536]{1,0:T(8,128)(2,1)S(1)}, bf16[48,1536]{1,0:T(8,128)(2,1)S(1)}, u32[]{:S(2)}, u32[]{:S(2)}) collective-permute-start(bf16[48,1536]{1,0:T(8,128)(2,1)S(1)} %get-tuple-element.73), channel_id=1, source_target_pairs={{8,0},{9,1},{10,2},{11,3},{12,4},{13,5},{14,6},{15,7},{0,8},{1,9},... | collective-permute-start | bytes 442376 | tf_op jit(solution)/shard_map/ppermute | solution.py:42
  183.1 2.7 %multiply_subtract_fusion = (f32[64,3072]{1,0:T(8,128)}, bf16[64,3072]{1,0:T(8,128)(2,1)}, f32[64,3072]{1,0:T(8,128)}) fusion(f32[64,3072]{1,0:T(8,128)S(1)} %copy-done.7, bf16[64,3072]{1,0:T(8,128)(2,1)S(1)} %collective-permute-done.25, bf16[2,64,3072]{2,1,0:T(8,128)(2,1)} %bitcast.23, s32[]{:T(128)S(6)} %select_n.72, bf16[64,3072]{1,0:T(8,128)(2,1)S(1)} %copy-done.9, ...), kind=kLoop, calls=%fused_computation.11 | loop fusion | flops 4128768 | bytes 4718596 | tf_op jit(solution)/shard_map/sub | solution.py:63
  185.9 4.4 %collective-permute-done.17.refs_3_ = bf16[48,1536]{1,0:T(8,128)(2,1)S(1)} collective-permute-done((bf16[48,1536]{1,0:T(8,128)(2,1)S(1)}, bf16[48,1536]{1,0:T(8,128)(2,1)S(1)}, u32[]{:S(2)}, u32[]{:S(2)}) %collective-permute-start.17) | collective-permute-done | bytes 147488 | tf_op jit(solution)/shard_map/ppermute | solution.py:42
  190.2 1.7 finish.1
  (91 shorter events, 4.4 us)
Async XLA Ops:
  7.2 103.7 %copy-start = (bf16[3072,8]{0,1:T(8,128)(2,1)S(1)}, bf16[3072,8]{0,1:T(8,128)(2,1)}, u32[]{:S(2)}) copy-start(bf16[3072,8]{0,1:T(8,128)(2,1)} %param.11) | copy-start | bytes 147460
  7.2 85.1 %all-gather.3.cloned.1.call-start = ((), (), s32[]{:S(2)}) async-start(), calls=%async_computation.1 | async-start | bytes 7077888 | tf_op jit(solution)/shard_map/all_gather | solution.py:235
  7.2 11.3 %collective-permute-start.7 = (bf16[192,1024]{1,0:T(8,128)(2,1)}, bf16[192,1024]{1,0:T(8,128)(2,1)S(1)}, u32[]{:S(2)}, u32[]{:S(2)}) collective-permute-start(bf16[192,1024]{1,0:T(8,128)(2,1)} %param.12), channel_id=1, source_target_pairs={{32,0},{48,16},{0,32},{16,48},{96,64},{112,80},{64,96},{80,112},{1... | collective-permute-start | bytes 1179656 | tf_op jit(solution)/shard_map/ppermute | solution.py:37
  19.6 1.4 copy-start.1
  19.6 1.4 copy-start.3
  20.6 13.0 %copy-start.10 = (bf16[64,3072]{1,0:T(8,128)(2,1)S(1)}, bf16[64,3072]{1,0:T(8,128)(2,1)}, u32[]{:S(2)}) copy-start(bf16[64,3072]{1,0:T(8,128)(2,1)} %param.13) | copy-start | bytes 1179652
  20.6 91.5 %all-gather.5.cloned.1.call-start = ((), (), s32[]{:S(2)}) async-start(), calls=%async_computation.2 | async-start | bytes 7077888 | tf_op jit(solution)/shard_map/all_gather | solution.py:235
  21.5 8.7 %collective-permute-start.3 = (bf16[48,3072]{1,0:T(8,128)(2,1)S(1)}, bf16[48,3072]{1,0:T(8,128)(2,1)S(1)}, u32[]{:S(2)}, u32[]{:S(2)}) collective-permute-start(bf16[48,3072]{1,0:T(8,128)(2,1)S(1)} %prep.1), channel_id=1, source_target_pairs={{1,0},{2,1},{3,2},{0,3},{5,4},{6,5},{7,6},{4,7},{9,8},{10,9},{11,1... | collective-permute-start | bytes 884744 | tf_op jit(solution)/shard_map/ppermute | solution.py:42
  24.6 9.0 %collective-permute-start.4 = (bf16[48,3072]{1,0:T(8,128)(2,1)S(1)}, bf16[48,3072]{1,0:T(8,128)(2,1)S(1)}, u32[]{:S(2)}, u32[]{:S(2)}) collective-permute-start(bf16[48,3072]{1,0:T(8,128)(2,1)S(1)} %prep.1), channel_id=1, source_target_pairs={{3,0},{0,1},{1,2},{2,3},{7,4},{4,5},{5,6},{6,7},{11,8},{8,9},{9,10... | collective-permute-start | bytes 884744 | tf_op jit(solution)/shard_map/ppermute | solution.py:42
  30.2 5.0 %copy-start.11 = (bf16[48,3072]{1,0:T(8,128)(2,1)}, bf16[48,3072]{1,0:T(8,128)(2,1)S(1)}, u32[]{:S(2)}) copy-start(bf16[48,3072]{1,0:T(8,128)(2,1)S(1)} %collective-permute-done.3) | copy-start | bytes 884740
  33.6 9.0 %collective-permute-start.10 = (bf16[64,3072]{1,0:T(8,128)(2,1)S(1)}, bf16[64,3072]{1,0:T(8,128)(2,1)S(1)}, u32[]{:S(2)}, u32[]{:S(2)}) collective-permute-start(bf16[64,3072]{1,0:T(8,128)(2,1)S(1)} %copy-done.10), channel_id=1, source_target_pairs={{32,0},{48,16},{0,32},{16,48},{96,64},{112,80},{64,96},{80,112},{1... | collective-permute-start | bytes 1179656 | tf_op jit(solution)/shard_map/ppermute | solution.py:37
  43.6 117.0 %reduce-scatter.2.cloned.1.call-start = ((), (), s32[]{:S(2)}) async-start(), calls=%async_computation.3 | async-start | bytes 7077888 | tf_op jit(solution)/shard_map/reduce_scatter | solution.py:260
  43.6 28.2 %collective-permute-start = (bf16[48,3072]{1,0:T(8,128)(2,1)S(1)}, bf16[48,3072]{1,0:T(8,128)(2,1)S(1)}, u32[]{:S(2)}, u32[]{:S(2)}) collective-permute-start(bf16[48,3072]{1,0:T(8,128)(2,1)S(1)} %prep.1), channel_id=1, source_target_pairs={{4,0},{5,1},{6,2},{7,3},{8,4},{9,5},{10,6},{11,7},{12,8},{13,9},{1... | collective-permute-start | bytes 884744 | tf_op jit(solution)/shard_map/ppermute | solution.py:42
  49.4 22.7 %collective-permute-start.1 = (bf16[48,3072]{1,0:T(8,128)(2,1)S(1)}, bf16[48,3072]{1,0:T(8,128)(2,1)S(1)}, u32[]{:S(2)}, u32[]{:S(2)}) collective-permute-start(bf16[48,3072]{1,0:T(8,128)(2,1)S(1)} %prep.1), channel_id=1, source_target_pairs={{12,0},{13,1},{14,2},{15,3},{0,4},{1,5},{2,6},{3,7},{4,8},{5,9},{6... | collective-permute-start | bytes 884744 | tf_op jit(solution)/shard_map/ppermute | solution.py:42
  49.4 22.9 %collective-permute-start.2 = (bf16[48,3072]{1,0:T(8,128)(2,1)S(1)}, bf16[48,3072]{1,0:T(8,128)(2,1)S(1)}, u32[]{:S(2)}, u32[]{:S(2)}) collective-permute-start(bf16[48,3072]{1,0:T(8,128)(2,1)S(1)} %prep.1), channel_id=1, source_target_pairs={{8,0},{9,1},{10,2},{11,3},{12,4},{13,5},{14,6},{15,7},{0,8},{1,9},... | collective-permute-start | bytes 884744 | tf_op jit(solution)/shard_map/ppermute | solution.py:42
  72.4 16.5 %collective-permute-start.6 = (bf16[144,3072]{1,0:T(8,128)(2,1)S(1)}, bf16[144,3072]{1,0:T(8,128)(2,1)S(1)}, u32[]{:S(2)}, u32[]{:S(2)}) collective-permute-start(bf16[144,3072]{1,0:T(8,128)(2,1)S(1)} %pad_maximum_fusion.3), channel_id=1, source_target_pairs={{3,0},{0,1},{1,2},{2,3},{7,4},{4,5},{5,6},{6,7},{11,8},{8,9},{9,10... | collective-permute-start | bytes 2654216 | tf_op jit(solution)/shard_map/ppermute | solution.py:42
  72.5 19.6 %collective-permute-start.5 = (bf16[144,3072]{1,0:T(8,128)(2,1)S(1)}, bf16[144,3072]{1,0:T(8,128)(2,1)S(1)}, u32[]{:S(2)}, u32[]{:S(2)}) collective-permute-start(bf16[144,3072]{1,0:T(8,128)(2,1)S(1)} %pad_maximum_fusion.3), channel_id=1, source_target_pairs={{1,0},{2,1},{3,2},{0,3},{5,4},{6,5},{7,6},{4,7},{9,8},{10,9},{11,1... | collective-permute-start | bytes 2654216 | tf_op jit(solution)/shard_map/ppermute | solution.py:42
  76.8 15.3 %copy-start.12 = (bf16[48,3072]{1,0:T(8,128)(2,1)S(1)}, bf16[48,3072]{1,0:T(8,128)(2,1)}, u32[]{:S(2)}) copy-start(bf16[48,3072]{1,0:T(8,128)(2,1)} %copy-done.11) | copy-start | bytes 884740
  92.3 16.1 %collective-permute-start.8 = (bf16[192,1536]{1,0:T(8,128)(2,1)S(1)}, bf16[192,1536]{1,0:T(8,128)(2,1)S(1)}, u32[]{:S(2)}, u32[]{:S(2)}) collective-permute-start(bf16[192,1536]{1,0:T(8,128)(2,1)S(1)} %slice.92), channel_id=1, source_target_pairs={{1,0},{2,1},{3,2},{0,3},{5,4},{6,5},{7,6},{4,7},{9,8},{10,9},{11,1... | collective-permute-start | bytes 1769480 | tf_op jit(solution)/shard_map/ppermute | solution.py:42
  94.8 6.7 %slice-start = ((s8[6291456]{0:T(1024)(128)(4,1)}), s8[4194304]{0:T(1024)(128)(4,1)S(1)}, s32[]{:S(2)}) async-start(s8[6291456]{0:T(1024)(128)(4,1)} %bitcast.17), calls=%async_computation.4 | async-start | bytes 8388608
  94.8 13.6 %collective-permute-start.9 = (bf16[192,1536]{1,0:T(8,128)(2,1)S(1)}, bf16[192,1536]{1,0:T(8,128)(2,1)S(1)}, u32[]{:S(2)}, u32[]{:S(2)}) collective-permute-start(bf16[192,1536]{1,0:T(8,128)(2,1)S(1)} %slice.93), channel_id=1, source_target_pairs={{3,0},{0,1},{1,2},{2,3},{7,4},{4,5},{5,6},{6,7},{11,8},{8,9},{9,10... | collective-permute-start | bytes 1769480 | tf_op jit(solution)/shard_map/ppermute | solution.py:42
  95.1 6.4 %slice-start.1 = ((s8[6291456]{0:T(1024)(128)(4,1)}), s8[2097152]{0:T(1024)(128)(4,1)S(1)}, s32[]{:S(2)}) async-start(s8[6291456]{0:T(1024)(128)(4,1)} %bitcast.17), calls=%async_computation.5 | async-start | bytes 4194304
  95.1 6.4 %copy-start.2 = (bf16[192,3072]{1,0:T(8,128)(2,1)S(1)}, bf16[192,3072]{1,0:T(8,128)(2,1)}, u32[]{:S(2)}) copy-start(bf16[192,3072]{1,0:T(8,128)(2,1)} %pad_maximum_fusion.refs_0_) | copy-start | bytes 3538948
  108.4 2.3 %copy-start.5 = (bf16[576,1024]{1,0:T(8,128)(2,1)}, bf16[576,1024]{1,0:T(8,128)(2,1)S(1)}, u32[]{:S(2)}) copy-start(bf16[576,1024]{1,0:T(8,128)(2,1)S(1)} %up.2.h_near) | copy-start | bytes 3538948
  110.7 1.3 copy-start.6
  112.1 2.8 %copy-start.4 = (bf16[1024,3072]{1,0:T(8,128)(2,1)S(1)}, bf16[1024,3072]{1,0:T(8,128)(2,1)}, u32[]{:S(2)}) copy-start(bf16[1024,3072]{1,0:T(8,128)(2,1)} %all-gather.5.cloned.1.call-done.d) | copy-start | bytes 18874372
  118.2 10.4 %collective-permute-start.18 = (bf16[192,768]{1,0:T(8,128)(2,1)S(1)}, bf16[192,768]{1,0:T(8,128)(2,1)S(1)}, u32[]{:S(2)}, u32[]{:S(2)}) collective-permute-start(bf16[192,768]{1,0:T(8,128)(2,1)S(1)} %get-tuple-element.71), channel_id=1, source_target_pairs={{3,0},{0,1},{1,2},{2,3},{7,4},{4,5},{5,6},{6,7},{11,8},{8,9},{9,10... | collective-permute-start | bytes 884744 | tf_op jit(solution)/shard_map/ppermute | solution.py:42
  119.7 10.0 %collective-permute-start.20 = (bf16[192,768]{1,0:T(8,128)(2,1)S(1)}, bf16[192,768]{1,0:T(8,128)(2,1)S(1)}, u32[]{:S(2)}, u32[]{:S(2)}) collective-permute-start(bf16[192,768]{1,0:T(8,128)(2,1)S(1)} %get-tuple-element.72), channel_id=1, source_target_pairs={{1,0},{2,1},{3,2},{0,3},{5,4},{6,5},{7,6},{4,7},{9,8},{10,9},{11,1... | collective-permute-start | bytes 884744 | tf_op jit(solution)/shard_map/ppermute | solution.py:42
  124.9 11.4 %collective-permute-start.11 = (bf16[192,768]{1,0:T(8,128)(2,1)S(1)}, bf16[192,768]{1,0:T(8,128)(2,1)S(1)}, u32[]{:S(2)}, u32[]{:S(2)}) collective-permute-start(bf16[192,768]{1,0:T(8,128)(2,1)S(1)} %get-tuple-element.77), channel_id=1, source_target_pairs={{3,0},{0,1},{1,2},{2,3},{7,4},{4,5},{5,6},{6,7},{11,8},{8,9},{9,10... | collective-permute-start | bytes 884744 | tf_op jit(solution)/shard_map/ppermute | solution.py:42
  125.5 11.1 %collective-permute-start.13 = (bf16[192,768]{1,0:T(8,128)(2,1)S(1)}, bf16[192,768]{1,0:T(8,128)(2,1)S(1)}, u32[]{:S(2)}, u32[]{:S(2)}) collective-permute-start(bf16[192,768]{1,0:T(8,128)(2,1)S(1)} %get-tuple-element.78), channel_id=1, source_target_pairs={{1,0},{2,1},{3,2},{0,3},{5,4},{6,5},{7,6},{4,7},{9,8},{10,9},{11,1... | collective-permute-start | bytes 884744 | tf_op jit(solution)/shard_map/ppermute | solution.py:42
  128.7 20.3 %collective-permute-start.19 = (bf16[192,1536]{1,0:T(8,128)(2,1)S(1)}, bf16[192,1536]{1,0:T(8,128)(2,1)S(1)}, u32[]{:S(2)}, u32[]{:S(2)}) collective-permute-start(bf16[192,1536]{1,0:T(8,128)(2,1)S(1)} %pad_maximum_fusion.8), channel_id=1, source_target_pairs={{3,0},{0,1},{1,2},{2,3},{7,4},{4,5},{5,6},{6,7},{11,8},{8,9},{9,10... | collective-permute-start | bytes 1769480 | tf_op jit(solution)/shard_map/ppermute | solution.py:42
  129.9 19.1 %collective-permute-start.21 = (bf16[192,1536]{1,0:T(8,128)(2,1)S(1)}, bf16[192,1536]{1,0:T(8,128)(2,1)S(1)}, u32[]{:S(2)}, u32[]{:S(2)}) collective-permute-start(bf16[192,1536]{1,0:T(8,128)(2,1)S(1)} %pad_maximum_fusion.9), channel_id=1, source_target_pairs={{1,0},{2,1},{3,2},{0,3},{5,4},{6,5},{7,6},{4,7},{9,8},{10,9},{11,1... | collective-permute-start | bytes 1769480 | tf_op jit(solution)/shard_map/ppermute | solution.py:42
  136.5 23.8 %collective-permute-start.12 = (bf16[192,1536]{1,0:T(8,128)(2,1)S(1)}, bf16[192,1536]{1,0:T(8,128)(2,1)S(1)}, u32[]{:S(2)}, u32[]{:S(2)}) collective-permute-start(bf16[192,1536]{1,0:T(8,128)(2,1)S(1)} %pad_maximum_fusion.6), channel_id=1, source_target_pairs={{3,0},{0,1},{1,2},{2,3},{7,4},{4,5},{5,6},{6,7},{11,8},{8,9},{9,10... | collective-permute-start | bytes 1769480 | tf_op jit(solution)/shard_map/ppermute | solution.py:42
  136.7 23.6 %collective-permute-start.14 = (bf16[192,1536]{1,0:T(8,128)(2,1)S(1)}, bf16[192,1536]{1,0:T(8,128)(2,1)S(1)}, u32[]{:S(2)}, u32[]{:S(2)}) collective-permute-start(bf16[192,1536]{1,0:T(8,128)(2,1)S(1)} %pad_maximum_fusion.7), channel_id=1, source_target_pairs={{1,0},{2,1},{3,2},{0,3},{5,4},{6,5},{7,6},{4,7},{9,8},{10,9},{11,1... | collective-permute-start | bytes 1769480 | tf_op jit(solution)/shard_map/ppermute | solution.py:42
  149.9 16.1 %collective-permute-start.24 = (bf16[48,1536]{1,0:T(8,128)(2,1)}, bf16[48,1536]{1,0:T(8,128)(2,1)S(1)}, u32[]{:S(2)}, u32[]{:S(2)}) collective-permute-start(bf16[48,1536]{1,0:T(8,128)(2,1)} %get-tuple-element.67), channel_id=1, source_target_pairs={{8,0},{9,1},{10,2},{11,3},{12,4},{13,5},{14,6},{15,7},{0,8},{1,9},... | collective-permute-start | bytes 442376 | tf_op jit(solution)/shard_map/ppermute | solution.py:42
  155.7 30.2 %collective-permute-start.22 = (bf16[48,1536]{1,0:T(8,128)(2,1)}, bf16[48,1536]{1,0:T(8,128)(2,1)S(1)}, u32[]{:S(2)}, u32[]{:S(2)}) collective-permute-start(bf16[48,1536]{1,0:T(8,128)(2,1)} %get-tuple-element.69), channel_id=1, source_target_pairs={{12,0},{13,1},{14,2},{15,3},{0,4},{1,5},{2,6},{3,7},{4,8},{5,9},{6... | collective-permute-start | bytes 442376 | tf_op jit(solution)/shard_map/ppermute | solution.py:42
  158.1 27.7 %collective-permute-start.23 = (bf16[48,1536]{1,0:T(8,128)(2,1)S(1)}, bf16[48,1536]{1,0:T(8,128)(2,1)S(1)}, u32[]{:S(2)}, u32[]{:S(2)}) collective-permute-start(bf16[48,1536]{1,0:T(8,128)(2,1)S(1)} %get-tuple-element.68), channel_id=1, source_target_pairs={{4,0},{5,1},{6,2},{7,3},{8,4},{9,5},{10,6},{11,7},{12,8},{13,9},{1... | collective-permute-start | bytes 442376 | tf_op jit(solution)/shard_map/ppermute | solution.py:42
  160.5 22.6 %copy-start.7 = (f32[64,3072]{1,0:T(8,128)S(1)}, f32[64,3072]{1,0:T(8,128)}, u32[]{:S(2)}) copy-start(f32[64,3072]{1,0:T(8,128)} %param.15) | copy-start | bytes 2359300
  160.5 22.6 %copy-start.8 = (f32[64,3072]{1,0:T(8,128)S(1)}, f32[64,3072]{1,0:T(8,128)}, u32[]{:S(2)}) copy-start(f32[64,3072]{1,0:T(8,128)} %param.17) | copy-start | bytes 2359300
  160.5 22.6 %copy-start.9 = (bf16[64,3072]{1,0:T(8,128)(2,1)S(1)}, bf16[64,3072]{1,0:T(8,128)(2,1)}, u32[]{:S(2)}) copy-start(bf16[64,3072]{1,0:T(8,128)(2,1)} %param.16) | copy-start | bytes 1179652
  161.7 19.2 %collective-permute-start.25 = (bf16[64,3072]{1,0:T(8,128)(2,1)S(1)}, bf16[64,3072]{1,0:T(8,128)(2,1)S(1)}, u32[]{:S(2)}, u32[]{:S(2)}) collective-permute-start(bf16[64,3072]{1,0:T(8,128)(2,1)S(1)} %dynamic-slice_bitcast_fusion), channel_id=1, source_target_pairs={{32,0},{48,16},{0,32},{16,48},{96,64},{112,80},{64,96},{80,112},{1... | collective-permute-start | bytes 1179656 | tf_op jit(solution)/shard_map/ppermute | solution.py:37
  163.8 22.1 %collective-permute-start.15 = (bf16[48,1536]{1,0:T(8,128)(2,1)S(1)}, bf16[48,1536]{1,0:T(8,128)(2,1)S(1)}, u32[]{:S(2)}, u32[]{:S(2)}) collective-permute-start(bf16[48,1536]{1,0:T(8,128)(2,1)S(1)} %get-tuple-element.75), channel_id=1, source_target_pairs={{12,0},{13,1},{14,2},{15,3},{0,4},{1,5},{2,6},{3,7},{4,8},{5,9},{6... | collective-permute-start | bytes 442376 | tf_op jit(solution)/shard_map/ppermute | solution.py:42
  166.1 19.8 %collective-permute-start.16 = (bf16[48,1536]{1,0:T(8,128)(2,1)S(1)}, bf16[48,1536]{1,0:T(8,128)(2,1)S(1)}, u32[]{:S(2)}, u32[]{:S(2)}) collective-permute-start(bf16[48,1536]{1,0:T(8,128)(2,1)S(1)} %get-tuple-element.74), channel_id=1, source_target_pairs={{4,0},{5,1},{6,2},{7,3},{8,4},{9,5},{10,6},{11,7},{12,8},{13,9},{1... | collective-permute-start | bytes 442376 | tf_op jit(solution)/shard_map/ppermute | solution.py:42
  181.0 9.3 %collective-permute-start.17 = (bf16[48,1536]{1,0:T(8,128)(2,1)S(1)}, bf16[48,1536]{1,0:T(8,128)(2,1)S(1)}, u32[]{:S(2)}, u32[]{:S(2)}) collective-permute-start(bf16[48,1536]{1,0:T(8,128)(2,1)S(1)} %get-tuple-element.73), channel_id=1, source_target_pairs={{8,0},{9,1},{10,2},{11,3},{12,4},{13,5},{14,6},{15,7},{0,8},{1,9},... | collective-permute-start | bytes 442376 | tf_op jit(solution)/shard_map/ppermute | solution.py:42
Sparse Core Ops, SparseCore 0:
  20.7 45.3 all-gather.2
  68.5 43.5 all-gather.4
  114.6 43.9 reduce-scatter.1

commit v2 on v1

--- a/solution.py
+++ b/solution.py
@@ -231,7 +231,8 @@
 
     def gathered(value):
         came = get_dp(value, zl=1)
-        pair = jnp.concatenate([jnp.where(zl == 0, value, came), jnp.where(zl == 0, came, value)], axis=0)
+        pair = jnp.concatenate([value, value], axis=0)
+        pair = lax.dynamic_update_slice_in_dim(pair, came, (1 - zl) * value.shape[0], axis=0)
         return lax.all_gather(pair, "dp", axis=0, tiled=True, axis_index_groups=groups)
 
     up = gathered(w_up)
@@ -272,7 +273,6 @@
     give = lax.dynamic_index_in_dim(x_sum, 1 - zl, axis=0, keepdims=False)
     grad_total = total([keep, get_dp(give, zl=1)])
     new_master, new_one, new_two = adam_step(grad_total, master, moment_one, moment_two)
-    owned[-1], new_master, new_one, new_two = tie((owned[-1], new_master, new_one, new_two))
     mixed = finish_call(routes, gating[:, None], owned)
     return (mixed, new_master, new_one, new_two)
 

time: 200 us -> 200 us (level)
  other arithmetic: 7.94 us -> 5.36 us
  starting transfers between devices: 55.4 us -> 57.8 us
    ppermute x3, waiting for transfers between devices: 28.7 us -> 15.4 us  [get_dp(): return lax.ppermute(value, 'dp', pairs)]
    ppermute x23, waiting for transfers between devices: 61.4 us -> 73 us  [get_tensor(): return lax.ppermute(value, 'tensor', pairs)]
    unnamed x31 -> x37, local copies, waits for them, and re-layouts: 3.36 us -> 4.93 us
  transfers between devices with their start and end apart: 29 -> 29, of which waited for: 15 -> 14; matrix products, arithmetic and copies ran while one was open for 8% -> 6% of each run, Pallas kernels for 8% -> 9%
where the time goes in v2:
time: 200 us; the launch traced here: 197 us
  waiting for transfers between devices  88.5 us (44%)
  starting transfers between devices  57.8 us (29%)
  Pallas kernels  17.8 us (9%)
  between operations  14.3 us (7%)
  local copies, waits for them, and re-layouts  13.3 us (7%)
  other arithmetic  5.36 us (3%)
    ppermute x23, waiting for transfers between devices, get_tensor(): return lax.ppermute(value, 'tensor', pairs)  73 us
    ppermute x23, starting transfers between devices, get_tensor(): return lax.ppermute(value, 'tensor', pairs)  51.6 us
    ppermute x3, waiting for transfers between devices, get_dp(): return lax.ppermute(value, 'dp', pairs)  15.4 us
    pallas_call x2, Pallas kernels, up_call(): pl.pallas_call(up_halves_kernel if halves else up_kernel, out_shape=jax.S...  9.15 us
    pallas_call x2, Pallas kernels, down_call(): pl.pallas_call(down_kernel, out_shape=[jax.ShapeDtypeStruct((192, 2 * wid...  6.5 us
    transpose x1, local copies, waits for them, and re-layouts, local(): grads.reshape(N_X, N_ZL, N_C, 64, D).transpose(0, 2, 1, 3, 4)  6.4 us
    ppermute x3, starting transfers between devices, get_dp(): return lax.ppermute(value, 'dp', pairs)  6.11 us
    unnamed x37, local copies, waits for them, and re-layouts  4.93 us
  transfers between devices with their start and end apart: 29, of which 14 were waited for; matrix products, arithmetic and copies ran while one was open for 6% of the time, Pallas kernels for 9%

profile of v2, /device:TPU:2, one launch (start us, length us, event | category | flops | bytes accessed | tf_op | source)
XLA Modules:
  0.0 197.3 jit_solution(5550799934323674007)
XLA Ops:
  7.2 2.0 %collective-permute-start.7 = (bf16[192,1024]{1,0:T(8,128)(2,1)}, bf16[192,1024]{1,0:T(8,128)(2,1)S(1)}, u32[]{:S(2)}, u32[]{:S(2)}) collective-permute-start(bf16[192,1024]{1,0:T(8,128)(2,1)} %param.12), channel_id=1, source_target_pairs={{32,0},{48,16},{0,32},{16,48},{96,64},{112,80},{64,96},{80,112},{1... | collective-permute-start | bytes 1179656 | tf_op jit(solution)/shard_map/ppermute | solution.py:37
  9.2 1.3 pad_maximum_fusion.4
  10.5 8.0 %collective-permute-done.7 = bf16[192,1024]{1,0:T(8,128)(2,1)S(1)} collective-permute-done((bf16[192,1024]{1,0:T(8,128)(2,1)}, bf16[192,1024]{1,0:T(8,128)(2,1)S(1)}, u32[]{:S(2)}, u32[]{:S(2)}) %collective-permute-start.7) | collective-permute-done | bytes 393248 | tf_op jit(solution)/shard_map/ppermute | solution.py:37
  18.6 0.9 copy-done.7
  19.6 0.4 prep.1
  20.0 3.1 %collective-permute-start.3 = (bf16[48,3072]{1,0:T(8,128)(2,1)S(1)}, bf16[48,3072]{1,0:T(8,128)(2,1)S(1)}, u32[]{:S(2)}, u32[]{:S(2)}) collective-permute-start(bf16[48,3072]{1,0:T(8,128)(2,1)S(1)} %prep.1), channel_id=1, source_target_pairs={{1,0},{2,1},{3,2},{0,3},{5,4},{6,5},{7,6},{4,7},{9,8},{10,9},{11,1... | collective-permute-start | bytes 884744 | tf_op jit(solution)/shard_map/ppermute | solution.py:42
  23.1 5.6 %collective-permute-done.3 = bf16[48,3072]{1,0:T(8,128)(2,1)S(1)} collective-permute-done((bf16[48,3072]{1,0:T(8,128)(2,1)S(1)}, bf16[48,3072]{1,0:T(8,128)(2,1)S(1)}, u32[]{:S(2)}, u32[]{:S(2)}) %collective-permute-start.3) | collective-permute-done | bytes 294944 | tf_op jit(solution)/shard_map/ppermute | solution.py:42
  28.7 3.4 %collective-permute-done.4 = bf16[48,3072]{1,0:T(8,128)(2,1)S(1)} collective-permute-done((bf16[48,3072]{1,0:T(8,128)(2,1)S(1)}, bf16[48,3072]{1,0:T(8,128)(2,1)S(1)}, u32[]{:S(2)}, u32[]{:S(2)}) %collective-permute-start.4) | collective-permute-done | bytes 294944 | tf_op jit(solution)/shard_map/ppermute | solution.py:42
  32.1 1.5 collective-permute-start.10
  33.7 7.3 %collective-permute-done.10 = bf16[64,3072]{1,0:T(8,128)(2,1)S(1)} collective-permute-done((bf16[64,3072]{1,0:T(8,128)(2,1)S(1)}, bf16[64,3072]{1,0:T(8,128)(2,1)S(1)}, u32[]{:S(2)}, u32[]{:S(2)}) %collective-permute-start.10) | collective-permute-done | bytes 393248 | tf_op jit(solution)/shard_map/ppermute | solution.py:37
  41.1 0.9 copy-done.8
  42.1 5.8 %collective-permute-start = (bf16[48,3072]{1,0:T(8,128)(2,1)S(1)}, bf16[48,3072]{1,0:T(8,128)(2,1)S(1)}, u32[]{:S(2)}, u32[]{:S(2)}) collective-permute-start(bf16[48,3072]{1,0:T(8,128)(2,1)S(1)} %prep.1), channel_id=1, source_target_pairs={{4,0},{5,1},{6,2},{7,3},{8,4},{9,5},{10,6},{11,7},{12,8},{13,9},{1... | collective-permute-start | bytes 884744 | tf_op jit(solution)/shard_map/ppermute | solution.py:42
  47.9 3.8 %collective-permute-start.2 = (bf16[48,3072]{1,0:T(8,128)(2,1)S(1)}, bf16[48,3072]{1,0:T(8,128)(2,1)S(1)}, u32[]{:S(2)}, u32[]{:S(2)}) collective-permute-start(bf16[48,3072]{1,0:T(8,128)(2,1)S(1)} %prep.1), channel_id=1, source_target_pairs={{8,0},{9,1},{10,2},{11,3},{12,4},{13,5},{14,6},{15,7},{0,8},{1,9},... | collective-permute-start | bytes 884744 | tf_op jit(solution)/shard_map/ppermute | solution.py:42
  51.7 18.6 %collective-permute-done = bf16[48,3072]{1,0:T(8,128)(2,1)S(1)} collective-permute-done((bf16[48,3072]{1,0:T(8,128)(2,1)S(1)}, bf16[48,3072]{1,0:T(8,128)(2,1)S(1)}, u32[]{:S(2)}, u32[]{:S(2)}) %collective-permute-start) | collective-permute-done | bytes 294944 | tf_op jit(solution)/shard_map/ppermute | solution.py:42
  70.3 0.4 collective-permute-done.1
  71.0 3.2 %collective-permute-start.5 = (bf16[144,3072]{1,0:T(8,128)(2,1)S(1)}, bf16[144,3072]{1,0:T(8,128)(2,1)S(1)}, u32[]{:S(2)}, u32[]{:S(2)}) collective-permute-start(bf16[144,3072]{1,0:T(8,128)(2,1)S(1)} %pad_maximum_fusion.3), channel_id=1, source_target_pairs={{1,0},{2,1},{3,2},{0,3},{5,4},{6,5},{7,6},{4,7},{9,8},{10,9},{11,1... | collective-permute-start | bytes 2654216 | tf_op jit(solution)/shard_map/ppermute | solution.py:42
  74.2 1.1 pad_maximum_fusion.refs_0_
  75.3 12.5 %collective-permute-done.6 = bf16[144,3072]{1,0:T(8,128)(2,1)S(1)} collective-permute-done((bf16[144,3072]{1,0:T(8,128)(2,1)S(1)}, bf16[144,3072]{1,0:T(8,128)(2,1)S(1)}, u32[]{:S(2)}, u32[]{:S(2)}) %collective-permute-start.6) | collective-permute-done | bytes 884768 | tf_op jit(solution)/shard_map/ppermute | solution.py:42
  87.9 2.2 %collective-permute-done.5 = bf16[144,3072]{1,0:T(8,128)(2,1)S(1)} collective-permute-done((bf16[144,3072]{1,0:T(8,128)(2,1)S(1)}, bf16[144,3072]{1,0:T(8,128)(2,1)S(1)}, u32[]{:S(2)}, u32[]{:S(2)}) %collective-permute-start.5) | collective-permute-done | bytes 884768 | tf_op jit(solution)/shard_map/ppermute | solution.py:42
  90.3 3.8 %collective-permute-start.8 = (bf16[192,1536]{1,0:T(8,128)(2,1)S(1)}, bf16[192,1536]{1,0:T(8,128)(2,1)S(1)}, u32[]{:S(2)}, u32[]{:S(2)}) collective-permute-start(bf16[192,1536]{1,0:T(8,128)(2,1)S(1)} %slice.92), channel_id=1, source_target_pairs={{1,0},{2,1},{3,2},{0,3},{5,4},{6,5},{7,6},{4,7},{9,8},{10,9},{11,1... | collective-permute-start | bytes 1769480 | tf_op jit(solution)/shard_map/ppermute | solution.py:42
  94.4 6.4 %copy.43 = bf16[4,2,2,64,3072]{4,3,2,1,0:T(8,128)(2,1)} copy(bf16[4,2,2,64,3072]{4,3,1,2,0:T(8,128)(2,1)} %bitcast.21) | data formatting | bytes 12582912 | tf_op jit(solution)/shard_map/transpose | solution.py:255
  100.8 6.9 %up.2.h_near = bf16[576,1024]{1,0:T(8,128)(2,1)S(1)} custom-call(bf16[192,3072]{1,0:T(8,128)(2,1)S(1)} %copy-done.2, bf16[192,3072]{1,0:T(8,128)(2,1)S(1)} %pad_maximum_fusion.1.refs_1_, bf16[192,3072]{1,0:T(8,128)(2,1)S(1)} %pad_maximum_fusion.2.refs_2_, bf16[3072,1024]{1,0:T(8,128)(2,1)S(1)} %bitcast.18), custom_call_target="tpu_custom_call" | custom-call | flops 3623878656 | bytes 11010048 | tf_op jit(solution)/shard_map/up/pallas_call | solution.py:172
  107.8 2.2 %up.3.h_far = bf16[192,1024]{1,0:T(8,128)(2,1)S(1)} custom-call(bf16[192,1536]{1,0:T(8,128)(2,1)S(1)} %collective-permute-done.8.left, bf16[192,1536]{1,0:T(8,128)(2,1)S(1)} %collective-permute-done.9.right, bf16[3072,1024]{1,0:T(8,128)(2,1)S(1)} %bitcast.18), custom_call_target="tpu_custom_call" | custom-call | flops 1207959552 | bytes 7864320 | tf_op jit(solution)/shard_map/up/pallas_call | solution.py:172
  110.2 0.3 fusion.7
  111.3 2.8 %copy-done.4 = bf16[1024,3072]{1,0:T(8,128)(2,1)S(1)} copy-done((bf16[1024,3072]{1,0:T(8,128)(2,1)S(1)}, bf16[1024,3072]{1,0:T(8,128)(2,1)}, u32[]{:S(2)}) %copy-start.4) | copy-done | bytes 6291480
  114.1 3.3 %down.3 = (bf16[192,1536]{1,0:T(8,128)(2,1)S(1)}, bf16[192,1536]{1,0:T(8,128)(2,1)S(1)}, bf16[192,1536]{1,0:T(8,128)(2,1)S(1)}, bf16[192,1536]{1,0:T(8,128)(2,1)S(1)}) custom-call(bf16[576,1024]{1,0:T(8,128)(2,1)S(1)} %copy-done.6, bf16[192,1024]{1,0:T(8,128)(2,1)S(1)} %up.3.h_far, bf16[1024,3072]{1,0:T(8,128)(2,1)S(1)} %copy-done.4), custom_call_target="tpu_custom_call" | custom-call | flops 2415919104 | bytes 7077888 | tf_op jit(solution)/shard_map/down/pallas_call | solution.py:194
  117.4 1.3 collective-permute-start.18
  118.7 2.1 %collective-permute-start.20 = (bf16[192,768]{1,0:T(8,128)(2,1)S(1)}, bf16[192,768]{1,0:T(8,128)(2,1)S(1)}, u32[]{:S(2)}, u32[]{:S(2)}) collective-permute-start(bf16[192,768]{1,0:T(8,128)(2,1)S(1)} %get-tuple-element.60), channel_id=1, source_target_pairs={{1,0},{2,1},{3,2},{0,3},{5,4},{6,5},{7,6},{4,7},{9,8},{10,9},{11,1... | collective-permute-start | bytes 884744 | tf_op jit(solution)/shard_map/ppermute | solution.py:42
  120.8 3.2 %down.2 = (bf16[192,1536]{1,0:T(8,128)(2,1)S(1)}, bf16[192,1536]{1,0:T(8,128)(2,1)S(1)}, bf16[192,1536]{1,0:T(8,128)(2,1)S(1)}, bf16[192,1536]{1,0:T(8,128)(2,1)S(1)}) custom-call(bf16[576,1024]{1,0:T(8,128)(2,1)S(1)} %copy-done.6, bf16[192,1024]{1,0:T(8,128)(2,1)S(1)} %up.3.h_far, bf16[1024,3072]{1,0:T(8,128)(2,1)S(1)} %copy-done.4), custom_call_target="tpu_custom_call" | custom-call | flops 2415919104 | bytes 7077888 | tf_op jit(solution)/shard_map/down/pallas_call | solution.py:194
  124.1 0.3 collective-permute-start.11
  124.4 3.3 %collective-permute-start.13 = (bf16[192,768]{1,0:T(8,128)(2,1)S(1)}, bf16[192,768]{1,0:T(8,128)(2,1)S(1)}, u32[]{:S(2)}, u32[]{:S(2)}) collective-permute-start(bf16[192,768]{1,0:T(8,128)(2,1)S(1)} %get-tuple-element.66), channel_id=1, source_target_pairs={{1,0},{2,1},{3,2},{0,3},{5,4},{6,5},{7,6},{4,7},{9,8},{10,9},{11,1... | collective-permute-start | bytes 884744 | tf_op jit(solution)/shard_map/ppermute | solution.py:42
  127.9 0.8 collective-permute-start.19
  128.8 2.6 %collective-permute-start.21 = (bf16[192,1536]{1,0:T(8,128)(2,1)S(1)}, bf16[192,1536]{1,0:T(8,128)(2,1)S(1)}, u32[]{:S(2)}, u32[]{:S(2)}) collective-permute-start(bf16[192,1536]{1,0:T(8,128)(2,1)S(1)} %pad_maximum_fusion.9), channel_id=1, source_target_pairs={{1,0},{2,1},{3,2},{0,3},{5,4},{6,5},{7,6},{4,7},{9,8},{10,9},{11,1... | collective-permute-start | bytes 1769480 | tf_op jit(solution)/shard_map/ppermute | solution.py:42
  131.4 4.1 %collective-permute-done.11 = bf16[192,768]{1,0:T(8,128)(2,1)S(1)} collective-permute-done((bf16[192,768]{1,0:T(8,128)(2,1)S(1)}, bf16[192,768]{1,0:T(8,128)(2,1)S(1)}, u32[]{:S(2)}, u32[]{:S(2)}) %collective-permute-start.11) | collective-permute-done | bytes 294944 | tf_op jit(solution)/shard_map/ppermute | solution.py:42
  135.9 3.3 %collective-permute-start.14 = (bf16[192,1536]{1,0:T(8,128)(2,1)S(1)}, bf16[192,1536]{1,0:T(8,128)(2,1)S(1)}, u32[]{:S(2)}, u32[]{:S(2)}) collective-permute-start(bf16[192,1536]{1,0:T(8,128)(2,1)S(1)} %pad_maximum_fusion.7), channel_id=1, source_target_pairs={{1,0},{2,1},{3,2},{0,3},{5,4},{6,5},{7,6},{4,7},{9,8},{10,9},{11,1... | collective-permute-start | bytes 1769480 | tf_op jit(solution)/shard_map/ppermute | solution.py:42
  139.2 9.0 %collective-permute-done.19 = bf16[192,1536]{1,0:T(8,128)(2,1)S(1)} collective-permute-done((bf16[192,1536]{1,0:T(8,128)(2,1)S(1)}, bf16[192,1536]{1,0:T(8,128)(2,1)S(1)}, u32[]{:S(2)}, u32[]{:S(2)}) %collective-permute-start.19) | collective-permute-done | bytes 589856 | tf_op jit(solution)/shard_map/ppermute | solution.py:42
  148.5 5.5 %collective-permute-start.22 = (bf16[48,1536]{1,0:T(8,128)(2,1)S(1)}, bf16[48,1536]{1,0:T(8,128)(2,1)S(1)}, u32[]{:S(2)}, u32[]{:S(2)}) collective-permute-start(bf16[48,1536]{1,0:T(8,128)(2,1)S(1)} %get-tuple-element.57), channel_id=1, source_target_pairs={{12,0},{13,1},{14,2},{15,3},{0,4},{1,5},{2,6},{3,7},{4,8},{5,9},{6... | collective-permute-start | bytes 442376 | tf_op jit(solution)/shard_map/ppermute | solution.py:42
  154.0 4.1 %collective-permute-start.24 = (bf16[48,1536]{1,0:T(8,128)(2,1)S(1)}, bf16[48,1536]{1,0:T(8,128)(2,1)S(1)}, u32[]{:S(2)}, u32[]{:S(2)}) collective-permute-start(bf16[48,1536]{1,0:T(8,128)(2,1)S(1)} %get-tuple-element.55), channel_id=1, source_target_pairs={{8,0},{9,1},{10,2},{11,3},{12,4},{13,5},{14,6},{15,7},{0,8},{1,9},... | collective-permute-start | bytes 442376 | tf_op jit(solution)/shard_map/ppermute | solution.py:42
  158.1 1.1 collective-permute-done.12
  159.5 1.0 dynamic-slice_bitcast_fusion
  160.5 2.6 %collective-permute-start.25 = (bf16[64,3072]{1,0:T(8,128)(2,1)S(1)}, bf16[64,3072]{1,0:T(8,128)(2,1)S(1)}, u32[]{:S(2)}, u32[]{:S(2)}) collective-permute-start(bf16[64,3072]{1,0:T(8,128)(2,1)S(1)} %dynamic-slice_bitcast_fusion), channel_id=1, source_target_pairs={{32,0},{48,16},{0,32},{16,48},{96,64},{112,80},{64,96},{80,112},{1... | collective-permute-start | bytes 1179656 | tf_op jit(solution)/shard_map/ppermute | solution.py:37
  163.1 1.7 collective-permute-start.15
  164.8 2.5 %collective-permute-start.16 = (bf16[48,1536]{1,0:T(8,128)(2,1)S(1)}, bf16[48,1536]{1,0:T(8,128)(2,1)S(1)}, u32[]{:S(2)}, u32[]{:S(2)}) collective-permute-start(bf16[48,1536]{1,0:T(8,128)(2,1)S(1)} %get-tuple-element.62), channel_id=1, source_target_pairs={{4,0},{5,1},{6,2},{7,3},{8,4},{9,5},{10,6},{11,7},{12,8},{13,9},{1... | collective-permute-start | bytes 442376 | tf_op jit(solution)/shard_map/ppermute | solution.py:42
  167.4 3.9 %collective-permute-start.17 = (bf16[48,1536]{1,0:T(8,128)(2,1)S(1)}, bf16[48,1536]{1,0:T(8,128)(2,1)S(1)}, u32[]{:S(2)}, u32[]{:S(2)}) collective-permute-start(bf16[48,1536]{1,0:T(8,128)(2,1)S(1)} %get-tuple-element.61), channel_id=1, source_target_pairs={{8,0},{9,1},{10,2},{11,3},{12,4},{13,5},{14,6},{15,7},{0,8},{1,9},... | collective-permute-start | bytes 442376 | tf_op jit(solution)/shard_map/ppermute | solution.py:42
  171.3 11.9 %collective-permute-done.15.refs_1_ = bf16[48,1536]{1,0:T(8,128)(2,1)S(1)} collective-permute-done((bf16[48,1536]{1,0:T(8,128)(2,1)S(1)}, bf16[48,1536]{1,0:T(8,128)(2,1)S(1)}, u32[]{:S(2)}, u32[]{:S(2)}) %collective-permute-start.15) | collective-permute-done | bytes 147488 | tf_op jit(solution)/shard_map/ppermute | solution.py:42
  183.2 4.0 %collective-permute-done.17.refs_3_ = bf16[48,1536]{1,0:T(8,128)(2,1)S(1)} collective-permute-done((bf16[48,1536]{1,0:T(8,128)(2,1)S(1)}, bf16[48,1536]{1,0:T(8,128)(2,1)S(1)}, u32[]{:S(2)}, u32[]{:S(2)}) %collective-permute-start.17) | collective-permute-done | bytes 147488 | tf_op jit(solution)/shard_map/ppermute | solution.py:42
  187.3 1.7 finish.1
  189.0 1.7 multiply_subtract_fusion
  (97 shorter events, 3.4 us)
Async XLA Ops:
  7.2 103.0 %copy-start = (bf16[3072,8]{0,1:T(8,128)(2,1)S(1)}, bf16[3072,8]{0,1:T(8,128)(2,1)}, u32[]{:S(2)}) copy-start(bf16[3072,8]{0,1:T(8,128)(2,1)} %param.11) | copy-start | bytes 147460
  7.2 83.0 %all-gather.3.cloned.1.call-start = ((), (), s32[]{:S(2)}) async-start(), calls=%async_computation.1 | async-start | bytes 7077888 | tf_op jit(solution)/shard_map/all_gather | solution.py:236
  7.2 11.3 %collective-permute-start.7 = (bf16[192,1024]{1,0:T(8,128)(2,1)}, bf16[192,1024]{1,0:T(8,128)(2,1)S(1)}, u32[]{:S(2)}, u32[]{:S(2)}) collective-permute-start(bf16[192,1024]{1,0:T(8,128)(2,1)} %param.12), channel_id=1, source_target_pairs={{32,0},{48,16},{0,32},{16,48},{96,64},{112,80},{64,96},{80,112},{1... | collective-permute-start | bytes 1179656 | tf_op jit(solution)/shard_map/ppermute | solution.py:37
  9.2 10.3 %copy-start.1 = (bf16[128,3072]{1,0:T(8,128)(2,1)S(1)}, bf16[128,3072]{1,0:T(8,128)(2,1)}, u32[]{:S(2)}) copy-start(bf16[128,3072]{1,0:T(8,128)(2,1)} %tokens.1) | copy-start | bytes 2359300
  9.2 10.3 %copy-start.3 = (s32[128,2]{0,1:T(2,128)S(1)}, s32[128,2]{0,1:T(2,128)}, u32[]{:S(2)}) copy-start(s32[128,2]{0,1:T(2,128)} %param.10) | copy-start | bytes 3076
  10.5 21.6 %copy-start.13 = (bf16[64,3072]{1,0:T(8,128)(2,1)S(1)}, bf16[64,3072]{1,0:T(8,128)(2,1)}, u32[]{:S(2)}) copy-start(bf16[64,3072]{1,0:T(8,128)(2,1)} %param.13) | copy-start | bytes 1179652
  18.6 0.9 copy-start.7
  19.5 91.5 %all-gather.5.cloned.1.call-start = ((), (), s32[]{:S(2)}) async-start(), calls=%async_computation.2 | async-start | bytes 7077888 | tf_op jit(solution)/shard_map/all_gather | solution.py:236
  20.0 8.7 %collective-permute-start.3 = (bf16[48,3072]{1,0:T(8,128)(2,1)S(1)}, bf16[48,3072]{1,0:T(8,128)(2,1)S(1)}, u32[]{:S(2)}, u32[]{:S(2)}) collective-permute-start(bf16[48,3072]{1,0:T(8,128)(2,1)S(1)} %prep.1), channel_id=1, source_target_pairs={{1,0},{2,1},{3,2},{0,3},{5,4},{6,5},{7,6},{4,7},{9,8},{10,9},{11,1... | collective-permute-start | bytes 884744 | tf_op jit(solution)/shard_map/ppermute | solution.py:42
  23.1 9.0 %collective-permute-start.4 = (bf16[48,3072]{1,0:T(8,128)(2,1)S(1)}, bf16[48,3072]{1,0:T(8,128)(2,1)S(1)}, u32[]{:S(2)}, u32[]{:S(2)}) collective-permute-start(bf16[48,3072]{1,0:T(8,128)(2,1)S(1)} %prep.1), channel_id=1, source_target_pairs={{3,0},{0,1},{1,2},{2,3},{7,4},{4,5},{5,6},{6,7},{11,8},{8,9},{9,10... | collective-permute-start | bytes 884744 | tf_op jit(solution)/shard_map/ppermute | solution.py:42
  28.7 5.0 %copy-start.14 = (bf16[48,3072]{1,0:T(8,128)(2,1)}, bf16[48,3072]{1,0:T(8,128)(2,1)S(1)}, u32[]{:S(2)}) copy-start(bf16[48,3072]{1,0:T(8,128)(2,1)S(1)} %collective-permute-done.3) | copy-start | bytes 884740
  32.1 9.0 %collective-permute-start.10 = (bf16[64,3072]{1,0:T(8,128)(2,1)S(1)}, bf16[64,3072]{1,0:T(8,128)(2,1)S(1)}, u32[]{:S(2)}, u32[]{:S(2)}) collective-permute-start(bf16[64,3072]{1,0:T(8,128)(2,1)S(1)} %copy-done.13), channel_id=1, source_target_pairs={{32,0},{48,16},{0,32},{16,48},{96,64},{112,80},{64,96},{80,112},{1... | collective-permute-start | bytes 1179656 | tf_op jit(solution)/shard_map/ppermute | solution.py:37
  41.1 0.9 copy-start.8
  42.0 117.4 %reduce-scatter.2.cloned.1.call-start = ((), (), s32[]{:S(2)}) async-start(), calls=%async_computation.3 | async-start | bytes 7077888 | tf_op jit(solution)/shard_map/reduce_scatter | solution.py:261
  42.1 28.2 %collective-permute-start = (bf16[48,3072]{1,0:T(8,128)(2,1)S(1)}, bf16[48,3072]{1,0:T(8,128)(2,1)S(1)}, u32[]{:S(2)}, u32[]{:S(2)}) collective-permute-start(bf16[48,3072]{1,0:T(8,128)(2,1)S(1)} %prep.1), channel_id=1, source_target_pairs={{4,0},{5,1},{6,2},{7,3},{8,4},{9,5},{10,6},{11,7},{12,8},{13,9},{1... | collective-permute-start | bytes 884744 | tf_op jit(solution)/shard_map/ppermute | solution.py:42
  47.9 22.7 %collective-permute-start.1 = (bf16[48,3072]{1,0:T(8,128)(2,1)S(1)}, bf16[48,3072]{1,0:T(8,128)(2,1)S(1)}, u32[]{:S(2)}, u32[]{:S(2)}) collective-permute-start(bf16[48,3072]{1,0:T(8,128)(2,1)S(1)} %prep.1), channel_id=1, source_target_pairs={{12,0},{13,1},{14,2},{15,3},{0,4},{1,5},{2,6},{3,7},{4,8},{5,9},{6... | collective-permute-start | bytes 884744 | tf_op jit(solution)/shard_map/ppermute | solution.py:42
  47.9 22.9 %collective-permute-start.2 = (bf16[48,3072]{1,0:T(8,128)(2,1)S(1)}, bf16[48,3072]{1,0:T(8,128)(2,1)S(1)}, u32[]{:S(2)}, u32[]{:S(2)}) collective-permute-start(bf16[48,3072]{1,0:T(8,128)(2,1)S(1)} %prep.1), channel_id=1, source_target_pairs={{8,0},{9,1},{10,2},{11,3},{12,4},{13,5},{14,6},{15,7},{0,8},{1,9},... | collective-permute-start | bytes 884744 | tf_op jit(solution)/shard_map/ppermute | solution.py:42
  70.9 17.0 %collective-permute-start.6 = (bf16[144,3072]{1,0:T(8,128)(2,1)S(1)}, bf16[144,3072]{1,0:T(8,128)(2,1)S(1)}, u32[]{:S(2)}, u32[]{:S(2)}) collective-permute-start(bf16[144,3072]{1,0:T(8,128)(2,1)S(1)} %pad_maximum_fusion.3), channel_id=1, source_target_pairs={{3,0},{0,1},{1,2},{2,3},{7,4},{4,5},{5,6},{6,7},{11,8},{8,9},{9,10... | collective-permute-start | bytes 2654216 | tf_op jit(solution)/shard_map/ppermute | solution.py:42
  71.0 19.1 %collective-permute-start.5 = (bf16[144,3072]{1,0:T(8,128)(2,1)S(1)}, bf16[144,3072]{1,0:T(8,128)(2,1)S(1)}, u32[]{:S(2)}, u32[]{:S(2)}) collective-permute-start(bf16[144,3072]{1,0:T(8,128)(2,1)S(1)} %pad_maximum_fusion.3), channel_id=1, source_target_pairs={{1,0},{2,1},{3,2},{0,3},{5,4},{6,5},{7,6},{4,7},{9,8},{10,9},{11,1... | collective-permute-start | bytes 2654216 | tf_op jit(solution)/shard_map/ppermute | solution.py:42
  75.3 14.8 %copy-start.15 = (bf16[48,3072]{1,0:T(8,128)(2,1)S(1)}, bf16[48,3072]{1,0:T(8,128)(2,1)}, u32[]{:S(2)}) copy-start(bf16[48,3072]{1,0:T(8,128)(2,1)} %copy-done.14) | copy-start | bytes 884740
  90.3 17.5 %collective-permute-start.8 = (bf16[192,1536]{1,0:T(8,128)(2,1)S(1)}, bf16[192,1536]{1,0:T(8,128)(2,1)S(1)}, u32[]{:S(2)}, u32[]{:S(2)}) collective-permute-start(bf16[192,1536]{1,0:T(8,128)(2,1)S(1)} %slice.92), channel_id=1, source_target_pairs={{1,0},{2,1},{3,2},{0,3},{5,4},{6,5},{7,6},{4,7},{9,8},{10,9},{11,1... | collective-permute-start | bytes 1769480 | tf_op jit(solution)/shard_map/ppermute | solution.py:42
  94.0 6.7 %slice-start = ((s8[6291456]{0:T(1024)(128)(4,1)}), s8[4194304]{0:T(1024)(128)(4,1)S(1)}, s32[]{:S(2)}) async-start(s8[6291456]{0:T(1024)(128)(4,1)} %bitcast.17), calls=%async_computation.4 | async-start | bytes 8388608
  94.1 13.7 %collective-permute-start.9 = (bf16[192,1536]{1,0:T(8,128)(2,1)S(1)}, bf16[192,1536]{1,0:T(8,128)(2,1)S(1)}, u32[]{:S(2)}, u32[]{:S(2)}) collective-permute-start(bf16[192,1536]{1,0:T(8,128)(2,1)S(1)} %slice.93), channel_id=1, source_target_pairs={{3,0},{0,1},{1,2},{2,3},{7,4},{4,5},{5,6},{6,7},{11,8},{8,9},{9,10... | collective-permute-start | bytes 1769480 | tf_op jit(solution)/shard_map/ppermute | solution.py:42
  94.3 6.4 %slice-start.1 = ((s8[6291456]{0:T(1024)(128)(4,1)}), s8[2097152]{0:T(1024)(128)(4,1)S(1)}, s32[]{:S(2)}) async-start(s8[6291456]{0:T(1024)(128)(4,1)} %bitcast.17), calls=%async_computation.5 | async-start | bytes 4194304
  94.4 6.4 %copy-start.2 = (bf16[192,3072]{1,0:T(8,128)(2,1)S(1)}, bf16[192,3072]{1,0:T(8,128)(2,1)}, u32[]{:S(2)}) copy-start(bf16[192,3072]{1,0:T(8,128)(2,1)} %pad_maximum_fusion.refs_0_) | copy-start | bytes 3538948
  107.7 2.3 %copy-start.5 = (bf16[576,1024]{1,0:T(8,128)(2,1)}, bf16[576,1024]{1,0:T(8,128)(2,1)S(1)}, u32[]{:S(2)}) copy-start(bf16[576,1024]{1,0:T(8,128)(2,1)S(1)} %up.2.h_near) | copy-start | bytes 3538948
  110.0 1.3 copy-start.6
  111.3 2.8 %copy-start.4 = (bf16[1024,3072]{1,0:T(8,128)(2,1)S(1)}, bf16[1024,3072]{1,0:T(8,128)(2,1)}, u32[]{:S(2)}) copy-start(bf16[1024,3072]{1,0:T(8,128)(2,1)} %all-gather.5.cloned.1.call-done.d) | copy-start | bytes 18874372
  117.4 10.4 %collective-permute-start.18 = (bf16[192,768]{1,0:T(8,128)(2,1)S(1)}, bf16[192,768]{1,0:T(8,128)(2,1)S(1)}, u32[]{:S(2)}, u32[]{:S(2)}) collective-permute-start(bf16[192,768]{1,0:T(8,128)(2,1)S(1)} %get-tuple-element.59), channel_id=1, source_target_pairs={{3,0},{0,1},{1,2},{2,3},{7,4},{4,5},{5,6},{6,7},{11,8},{8,9},{9,10... | collective-permute-start | bytes 884744 | tf_op jit(solution)/shard_map/ppermute | solution.py:42
  118.7 10.0 %collective-permute-start.20 = (bf16[192,768]{1,0:T(8,128)(2,1)S(1)}, bf16[192,768]{1,0:T(8,128)(2,1)S(1)}, u32[]{:S(2)}, u32[]{:S(2)}) collective-permute-start(bf16[192,768]{1,0:T(8,128)(2,1)S(1)} %get-tuple-element.60), channel_id=1, source_target_pairs={{1,0},{2,1},{3,2},{0,3},{5,4},{6,5},{7,6},{4,7},{9,8},{10,9},{11,1... | collective-permute-start | bytes 884744 | tf_op jit(solution)/shard_map/ppermute | solution.py:42
  124.1 11.5 %collective-permute-start.11 = (bf16[192,768]{1,0:T(8,128)(2,1)S(1)}, bf16[192,768]{1,0:T(8,128)(2,1)S(1)}, u32[]{:S(2)}, u32[]{:S(2)}) collective-permute-start(bf16[192,768]{1,0:T(8,128)(2,1)S(1)} %get-tuple-element.65), channel_id=1, source_target_pairs={{3,0},{0,1},{1,2},{2,3},{7,4},{4,5},{5,6},{6,7},{11,8},{8,9},{9,10... | collective-permute-start | bytes 884744 | tf_op jit(solution)/shard_map/ppermute | solution.py:42
  124.4 11.3 %collective-permute-start.13 = (bf16[192,768]{1,0:T(8,128)(2,1)S(1)}, bf16[192,768]{1,0:T(8,128)(2,1)S(1)}, u32[]{:S(2)}, u32[]{:S(2)}) collective-permute-start(bf16[192,768]{1,0:T(8,128)(2,1)S(1)} %get-tuple-element.66), channel_id=1, source_target_pairs={{1,0},{2,1},{3,2},{0,3},{5,4},{6,5},{7,6},{4,7},{9,8},{10,9},{11,1... | collective-permute-start | bytes 884744 | tf_op jit(solution)/shard_map/ppermute | solution.py:42
  127.9 20.3 %collective-permute-start.19 = (bf16[192,1536]{1,0:T(8,128)(2,1)S(1)}, bf16[192,1536]{1,0:T(8,128)(2,1)S(1)}, u32[]{:S(2)}, u32[]{:S(2)}) collective-permute-start(bf16[192,1536]{1,0:T(8,128)(2,1)S(1)} %pad_maximum_fusion.8), channel_id=1, source_target_pairs={{3,0},{0,1},{1,2},{2,3},{7,4},{4,5},{5,6},{6,7},{11,8},{8,9},{9,10... | collective-permute-start | bytes 1769480 | tf_op jit(solution)/shard_map/ppermute | solution.py:42
  128.8 19.4 %collective-permute-start.21 = (bf16[192,1536]{1,0:T(8,128)(2,1)S(1)}, bf16[192,1536]{1,0:T(8,128)(2,1)S(1)}, u32[]{:S(2)}, u32[]{:S(2)}) collective-permute-start(bf16[192,1536]{1,0:T(8,128)(2,1)S(1)} %pad_maximum_fusion.9), channel_id=1, source_target_pairs={{1,0},{2,1},{3,2},{0,3},{5,4},{6,5},{7,6},{4,7},{9,8},{10,9},{11,1... | collective-permute-start | bytes 1769480 | tf_op jit(solution)/shard_map/ppermute | solution.py:42
  135.7 23.5 %collective-permute-start.12 = (bf16[192,1536]{1,0:T(8,128)(2,1)S(1)}, bf16[192,1536]{1,0:T(8,128)(2,1)S(1)}, u32[]{:S(2)}, u32[]{:S(2)}) collective-permute-start(bf16[192,1536]{1,0:T(8,128)(2,1)S(1)} %pad_maximum_fusion.6), channel_id=1, source_target_pairs={{3,0},{0,1},{1,2},{2,3},{7,4},{4,5},{5,6},{6,7},{11,8},{8,9},{9,10... | collective-permute-start | bytes 1769480 | tf_op jit(solution)/shard_map/ppermute | solution.py:42
  135.9 23.3 %collective-permute-start.14 = (bf16[192,1536]{1,0:T(8,128)(2,1)S(1)}, bf16[192,1536]{1,0:T(8,128)(2,1)S(1)}, u32[]{:S(2)}, u32[]{:S(2)}) collective-permute-start(bf16[192,1536]{1,0:T(8,128)(2,1)S(1)} %pad_maximum_fusion.7), channel_id=1, source_target_pairs={{1,0},{2,1},{3,2},{0,3},{5,4},{6,5},{7,6},{4,7},{9,8},{10,9},{11,1... | collective-permute-start | bytes 1769480 | tf_op jit(solution)/shard_map/ppermute | solution.py:42
  148.5 16.4 %collective-permute-start.22 = (bf16[48,1536]{1,0:T(8,128)(2,1)S(1)}, bf16[48,1536]{1,0:T(8,128)(2,1)S(1)}, u32[]{:S(2)}, u32[]{:S(2)}) collective-permute-start(bf16[48,1536]{1,0:T(8,128)(2,1)S(1)} %get-tuple-element.57), channel_id=1, source_target_pairs={{12,0},{13,1},{14,2},{15,3},{0,4},{1,5},{2,6},{3,7},{4,8},{5,9},{6... | collective-permute-start | bytes 442376 | tf_op jit(solution)/shard_map/ppermute | solution.py:42
  154.0 13.4 %collective-permute-start.23 = (bf16[48,1536]{1,0:T(8,128)(2,1)S(1)}, bf16[48,1536]{1,0:T(8,128)(2,1)S(1)}, u32[]{:S(2)}, u32[]{:S(2)}) collective-permute-start(bf16[48,1536]{1,0:T(8,128)(2,1)S(1)} %get-tuple-element.56), channel_id=1, source_target_pairs={{4,0},{5,1},{6,2},{7,3},{8,4},{9,5},{10,6},{11,7},{12,8},{13,9},{1... | collective-permute-start | bytes 442376 | tf_op jit(solution)/shard_map/ppermute | solution.py:42
  154.0 17.3 %collective-permute-start.24 = (bf16[48,1536]{1,0:T(8,128)(2,1)S(1)}, bf16[48,1536]{1,0:T(8,128)(2,1)S(1)}, u32[]{:S(2)}, u32[]{:S(2)}) collective-permute-start(bf16[48,1536]{1,0:T(8,128)(2,1)S(1)} %get-tuple-element.55), channel_id=1, source_target_pairs={{8,0},{9,1},{10,2},{11,3},{12,4},{13,5},{14,6},{15,7},{0,8},{1,9},... | collective-permute-start | bytes 442376 | tf_op jit(solution)/shard_map/ppermute | solution.py:42
  160.5 28.5 %collective-permute-start.25 = (bf16[64,3072]{1,0:T(8,128)(2,1)S(1)}, bf16[64,3072]{1,0:T(8,128)(2,1)S(1)}, u32[]{:S(2)}, u32[]{:S(2)}) collective-permute-start(bf16[64,3072]{1,0:T(8,128)(2,1)S(1)} %dynamic-slice_bitcast_fusion), channel_id=1, source_target_pairs={{32,0},{48,16},{0,32},{16,48},{96,64},{112,80},{64,96},{80,112},{1... | collective-permute-start | bytes 1179656 | tf_op jit(solution)/shard_map/ppermute | solution.py:37
  163.1 25.9 %copy-start.11 = (bf16[128,3072]{1,0:T(8,128)(2,1)S(1)}, bf16[128,3072]{1,0:T(8,128)(2,1)}, u32[]{:S(2)}) copy-start(bf16[128,3072]{1,0:T(8,128)(2,1)} %reduce-scatter.2.cloned.1.call-done) | copy-start | bytes 2359300
  163.1 25.9 %copy-start.9 = (f32[64,3072]{1,0:T(8,128)S(1)}, f32[64,3072]{1,0:T(8,128)}, u32[]{:S(2)}) copy-start(f32[64,3072]{1,0:T(8,128)} %param.15) | copy-start | bytes 2359300
  163.1 25.9 %copy-start.10 = (f32[64,3072]{1,0:T(8,128)S(1)}, f32[64,3072]{1,0:T(8,128)}, u32[]{:S(2)}) copy-start(f32[64,3072]{1,0:T(8,128)} %param.17) | copy-start | bytes 2359300
  163.1 25.9 %copy-start.12 = (bf16[64,3072]{1,0:T(8,128)(2,1)S(1)}, bf16[64,3072]{1,0:T(8,128)(2,1)}, u32[]{:S(2)}) copy-start(bf16[64,3072]{1,0:T(8,128)(2,1)} %param.16) | copy-start | bytes 1179652
  163.1 20.1 %collective-permute-start.15 = (bf16[48,1536]{1,0:T(8,128)(2,1)S(1)}, bf16[48,1536]{1,0:T(8,128)(2,1)S(1)}, u32[]{:S(2)}, u32[]{:S(2)}) collective-permute-start(bf16[48,1536]{1,0:T(8,128)(2,1)S(1)} %get-tuple-element.63), channel_id=1, source_target_pairs={{12,0},{13,1},{14,2},{15,3},{0,4},{1,5},{2,6},{3,7},{4,8},{5,9},{6... | collective-permute-start | bytes 442376 | tf_op jit(solution)/shard_map/ppermute | solution.py:42
  164.8 18.4 %collective-permute-start.16 = (bf16[48,1536]{1,0:T(8,128)(2,1)S(1)}, bf16[48,1536]{1,0:T(8,128)(2,1)S(1)}, u32[]{:S(2)}, u32[]{:S(2)}) collective-permute-start(bf16[48,1536]{1,0:T(8,128)(2,1)S(1)} %get-tuple-element.62), channel_id=1, source_target_pairs={{4,0},{5,1},{6,2},{7,3},{8,4},{9,5},{10,6},{11,7},{12,8},{13,9},{1... | collective-permute-start | bytes 442376 | tf_op jit(solution)/shard_map/ppermute | solution.py:42
  167.4 19.9 %collective-permute-start.17 = (bf16[48,1536]{1,0:T(8,128)(2,1)S(1)}, bf16[48,1536]{1,0:T(8,128)(2,1)S(1)}, u32[]{:S(2)}, u32[]{:S(2)}) collective-permute-start(bf16[48,1536]{1,0:T(8,128)(2,1)S(1)} %get-tuple-element.61), channel_id=1, source_target_pairs={{8,0},{9,1},{10,2},{11,3},{12,4},{13,5},{14,6},{15,7},{0,8},{1,9},... | collective-permute-start | bytes 442376 | tf_op jit(solution)/shard_map/ppermute | solution.py:42
Sparse Core Ops, SparseCore 0:
  19.6 45.3 all-gather.2
  67.4 43.5 all-gather.4
  113.5 43.9 reduce-scatter.1
